TPU v7x, 1024 devices: a whole 8x8x8 slice. The times are simulated.
1024 devices in a mesh: branch: 64 (over y, x), leaf: 16 (over z, core).
Axes of the slice: x: 8, y: 8, z: 8, core: 2. Of those that a mesh axis runs over, the one named last changes fastest.
Arguments:
- vectors: bfloat16 [16, 1048576], P(None, ('branch', 'leaf')), may hold values from -6 to 6
- near_ids: int32 [16384, 8], P(('branch', 'leaf')), may hold values from 0 to 16383, as said below
- coup_ids: int32 [16384, 8], P(('branch', 'leaf')), may hold values from 0 to 16383, as said below
- near_blocks: bfloat16 [16384, 8, 4096], P(('branch', 'leaf')), may hold values from -0.25 to 0.25
- coup_blocks: bfloat16 [16384, 8, 4096], P(('branch', 'leaf')), may hold values from -0.25 to 0.25
- col_basis: bfloat16 [16384, 4096], P(('branch', 'leaf')), may hold values from -0.75 to 0.75
- row_basis: bfloat16 [16384, 4096], P(('branch', 'leaf')), may hold values from -0.5 to 0.5
- col_transfer: bfloat16 [16384, 4096], P(('branch', 'leaf')), may hold values from -0.046875 to 0.046875
- row_transfer: bfloat16 [16384, 4096], P(('branch', 'leaf')), may hold values from -0.75 to 0.75
- top_coupling: float32 [64, 64, 4096], P('branch'), may hold values from -0.09375 to 0.09375
Outputs:
- product: float32 [16, 1048576], P(None, ('branch', 'leaf'))
Inputs may be any that keep to these rules, and one draw needn't show every extreme that they name: Leaf g lies on device g // 16 (branch index major, leaf index minor). Entry 0 of row i of near_ids is i; every other entry of near_ids names a leaf whose device has the same leaf index as row i's device and a branch index equal to it or one away cyclically. Over near_ids and coup_ids together, the rows of one device name at most 4 distinct leaves of any one other device; some device names exactly 4 of one peer in every draw. `coup_ids`: every entry names a leaf whose device has the same leaf index as row i's device and a branch index two or more away cyclically; the bound of 4 distinct leaves a device pair stated for near_ids covers both lists together.
All inputs are finite; a program needn't handle non-finite values.
Results may differ from a plain program's by a relative error of at most 0.0034.
Values may be sent and summed in bfloat16 or wider, within the bound.
No kernel may reach another device: no remote copies, remote signals or barrier semaphores. Data moves between devices by JAX's collectives and lax.ppermute only.
A program may use at most 32 MiB of HBM per device.

v0:
```python
import jax
import jax.numpy as jnp
from jax import lax
from jax.sharding import PartitionSpec as P

LEAF = 64
RANK = 64
NEAR = 8
COUP = 8


def gather_rows(table, places):
    picked = jnp.take(table, places.reshape(-1), axis=0)
    return picked.reshape(places.shape + (table.shape[1],))


def body(
    vectors,
    near_ids,
    coup_ids,
    near_blocks,
    coup_blocks,
    col_basis,
    row_basis,
    col_transfer,
    row_transfer,
    top_coupling,
):
    rhs_count = vectors.shape[0]
    local_count = near_ids.shape[0]
    branches = lax.axis_size("branch")
    columns = lax.axis_size("leaf")
    leaf_vectors = vectors.reshape(rhs_count, local_count, LEAF).transpose(1, 0, 2)
    basis_in = col_basis.reshape(local_count, LEAF, RANK)
    coeffs = jnp.einsum(
        "lpk,lrp->lrk", basis_in, leaf_vectors, preferred_element_type=jnp.float32
    ).astype(jnp.bfloat16)
    flat_vectors = leaf_vectors.reshape(local_count, rhs_count * LEAF)
    flat_coeffs = coeffs.reshape(local_count, rhs_count * RANK)
    all_ids = jnp.concatenate([near_ids, coup_ids], axis=1)
    owners = all_ids // (columns * local_count)
    within = all_ids % local_count
    table_vectors, table_coeffs = (
        lax.all_gather(flat_vectors, "branch", axis=0, tiled=True),
        lax.all_gather(flat_coeffs, "branch", axis=0, tiled=True),
    )
    places = owners * local_count + within
    near_places = places[:, :NEAR]
    coup_places = places[:, NEAR:]
    transfer_up = col_transfer.reshape(local_count, RANK, RANK)
    partial_root = jnp.einsum(
        "lkc,lrk->rc", transfer_up, coeffs, preferred_element_type=jnp.float32
    )[None]
    top_rows = top_coupling.reshape(branches, RANK, RANK)
    folded = jnp.einsum(
        "mac,mrc->ra",
        top_rows,
        lax.all_gather(partial_root, "branch", axis=0, tiled=True),
        precision=lax.Precision.HIGHEST,
    )
    near_vectors = gather_rows(table_vectors, near_places).reshape(
        local_count, NEAR, rhs_count, LEAF
    )
    blocks_near = near_blocks.reshape(local_count, NEAR, LEAF, LEAF)
    near_terms = jnp.einsum(
        "inpq,inrq->irp", blocks_near, near_vectors, preferred_element_type=jnp.float32
    )
    far_coeffs = gather_rows(table_coeffs, coup_places).reshape(local_count, COUP, rhs_count, RANK)
    blocks_coup = coup_blocks.reshape(local_count, COUP, RANK, RANK)
    coupled = jnp.einsum(
        "inab,inrb->ira", blocks_coup, far_coeffs, preferred_element_type=jnp.float32
    )
    top_coeffs = lax.psum(folded, "leaf").astype(jnp.bfloat16)
    transfer_down = row_transfer.reshape(local_count, RANK, RANK)
    inner_terms = coupled + jnp.einsum(
        "iac,rc->ira", transfer_down, top_coeffs, preferred_element_type=jnp.float32
    )
    inner_terms = inner_terms.astype(jnp.bfloat16)
    basis_out = row_basis.reshape(local_count, LEAF, RANK)
    output_terms = near_terms + jnp.einsum(
        "ipa,ira->irp", basis_out, inner_terms, preferred_element_type=jnp.float32
    )
    return output_terms.transpose(1, 0, 2).reshape(rhs_count, local_count * LEAF)


def solution(mesh):
    in_specs = (
        P(None, ("branch", "leaf")),
        P(("branch", "leaf"), None),
        P(("branch", "leaf"), None),
        P(("branch", "leaf"), None, None),
        P(("branch", "leaf"), None, None),
        P(("branch", "leaf"), None),
        P(("branch", "leaf"), None),
        P(("branch", "leaf"), None),
        P(("branch", "leaf"), None),
        P("branch", None, None),
    )
    out_specs = P(None, ("branch", "leaf"))
    return jax.shard_map(body, mesh=mesh, in_specs=in_specs, out_specs=out_specs, check_vma=False)
```

profile of v0, /device:TPU:1, one launch (start us, length us, event | category | flops | bytes accessed | tf_op | source)
XLA Modules:
  0.0 214.8 jit_solution(4197406985033954863)
XLA Ops:
  6.5 0.0 all-gather.6.cloned.1.call-start
  6.5 0.9 reshape.44
  7.4 1.2 reshape.48
  8.6 0.0 copy-start.3
  8.6 0.2 convolution_convert_fusion
  8.8 0.0 copy-start.1
  8.8 0.7 reshape.49
  9.5 0.0 all-gather.6.cloned.1.call-update
  9.6 0.0 all-gather.4.cloned.1.call-start
  9.6 0.7 reshape.45
  10.4 0.0 all-gather.4.cloned.1.call-update
  10.4 0.7 constant_dynamic-update-slice_fusion.1
  11.1 0.7 constant_dynamic-update-slice_fusion
  11.8 0.1 copy.16
  11.9 0.1 reshape.50
  12.0 4.2 %reshape.51 = bf16[16,8,64,64]{3,2,1,0:T(8,128)(2,1)} reshape(bf16[16,8,4096]{2,1,0:T(8,128)(2,1)} %param.16) | data formatting | bytes 2097152 | tf_op jit(solution)/shard_map/reshape | solution.py:69
  16.2 0.0 copy-done.3
  16.2 0.2 reshape.52
  16.4 0.0 copy-done.1
  16.4 0.8 reshape.53
  17.3 1.9 reshape.54
  19.2 1.9 reshape.55
  21.1 0.1 copy.14
  21.2 0.1 reshape.46
  21.3 4.3 %reshape.47 = bf16[16,8,64,64]{3,2,1,0:T(8,128)(2,1)} reshape(bf16[16,8,4096]{2,1,0:T(8,128)(2,1)} %param.15) | data formatting | bytes 2097152 | tf_op jit(solution)/shard_map/reshape | solution.py:64
  25.6 0.2 convolution_bitcast_fusion.3
  25.8 42.1 %all-gather = f32[1024,64]{1,0:T(8,128)S(1)} all-gather(f32[16,64]{1,0:T(8,128)S(1)} %convolution_bitcast_fusion.3), channel_id=2, replica_groups=mesh['branch'=64,'leaf'=16] {'branch'}, dimensions={0}, use_global_device_ids=true | all-gather | bytes 266240 | tf_op jit(solution)/shard_map/all_gather | solution.py:58
  67.9 1.7 convolution_bitcast_fusion.4
  69.6 47.6 %psum.7 = bf16[16,64]{1,0:T(8,128)(2,1)S(1)} all-reduce(f32[16,64]{1,0:T(8,128)S(1)} %convolution_bitcast_fusion.4), channel_id=1, replica_groups=mesh['branch'=64,'leaf'=16] {'leaf'}, use_global_device_ids=true, to_apply=%region_0.2 | all-reduce | flops 1024 | bytes 6144 | tf_op jit(solution)/shard_map/psum | solution.py:73
  117.3 0.0 all-gather.6.cloned.1.call-done
  117.3 2.9 %gather_fusion.1 = bf16[128,1024]{1,0:T(8,128)(2,1)S(1)} fusion(bf16[1024,1024]{1,0:T(8,128)(2,1)} %all-gather.6.cloned.1.call-done, s32[1024]{0:T(1024)S(1)} %pad_clamp_fusion), kind=kCustom, calls=%fused_computation.1.clone | custom fusion | bytes 524800 | tf_op jit(solution)/shard_map/jit(_take)/gather | solution.py:13
  120.2 0.1 broadcast_select_fusion
  120.3 0.0 copy-start
  120.3 0.3 reshape_reshape.7
  120.7 78.5 %all-gather.4.cloned.1.call-done = bf16[1024,1024]{1,0:T(8,128)(2,1)} async-done(((bf16[16,1024]{1,0:T(8,128)(2,1)}), bf16[1024,1024]{1,0:T(8,128)(2,1)}) %all-gather.4.cloned.1.call-update) | async-done | bytes 2097168 | tf_op jit(solution)/shard_map/all_gather | solution.py:44
  199.2 2.9 %gather_fusion = bf16[128,1024]{1,0:T(8,128)(2,1)S(1)} fusion(bf16[1024,1024]{1,0:T(8,128)(2,1)} %all-gather.4.cloned.1.call-done, s32[1024]{0:T(1024)S(1)} %pad_clamp_fusion.1), kind=kCustom, calls=%fused_computation.clone | custom fusion | bytes 524800 | tf_op jit(solution)/shard_map/jit(_take)/gather | solution.py:13
  202.1 0.1 broadcast_select_fusion.1
  202.2 0.3 reshape_reshape.6
  202.6 0.0 copy-done
  202.6 0.0 copy-start.2
  202.6 0.6 convolution_bitcast_fusion
  203.2 0.3 copy-done.2
  203.5 1.4 fusion.4
  204.9 2.3 %fusion.2 = f32[16,16,64]{2,0,1:T(8,128)S(1)} fusion(f32[16,16,64]{2,1,0:T(8,128)S(1)} %fusion.4, bf16[16,8,16,64]{3,2,1,0:T(8,128)(2,1)S(1)} %reshape_reshape.6, bf16[16,8,64,64]{3,2,1,0:T(8,128)(2,1)} %reshape.47), kind=kOutput, calls=%fused_computation.7 | convolution fusion | flops 16793600 | bytes 1441792 | tf_op jit(solution)/shard_map/inpq,inrq->irp/dot_general | solution.py:65
  207.2 0.1 copy.17
  207.2 0.7 reshape.56
  (9 shorter events, 0.1 us)
Async XLA Ops:
  6.5 110.8 %all-gather.6.cloned.1.call-start = ((), (), s32[]{:S(2)}) async-start(), calls=%async_computation.1 | async-start | bytes 2129920 | tf_op jit(solution)/shard_map/all_gather | solution.py:45
  8.6 7.6 %copy-start.3 = (bf16[16,4096]{1,0:T(8,128)(2,1)S(1)}, bf16[16,4096]{1,0:T(8,128)(2,1)}, u32[]{:S(2)}) copy-start(bf16[16,4096]{1,0:T(8,128)(2,1)} %param.19) | copy-start | bytes 393220
  8.8 7.6 %copy-start.1 = (f32[1,64,4096]{2,1,0:T(8,128)S(1)}, f32[1,64,4096]{2,1,0:T(8,128)}, u32[]{:S(2)}) copy-start(f32[1,64,4096]{2,1,0:T(8,128)} %param.21) | copy-start | bytes 3145732
  9.6 189.6 %all-gather.4.cloned.1.call-start = ((), (), s32[]{:S(2)}) async-start(), calls=%async_computation | async-start | bytes 2129920 | tf_op jit(solution)/shard_map/all_gather | solution.py:44
  120.3 82.2 %copy-start = (bf16[16,8,64,64]{3,2,1,0:T(8,128)(2,1)S(1)}, bf16[16,8,64,64]{3,2,1,0:T(8,128)(2,1)}, u32[]{:S(2)}) copy-start(bf16[16,8,64,64]{3,2,1,0:T(8,128)(2,1)} %reshape.51) | copy-start | bytes 3145732
  202.6 1.0 copy-start.2
Sparse Core Ops, SparseCore 0:
  11.6 96.4 all-gather.5
  112.3 86.8 all-gather.3
where the time goes:
time: 218 us; the launch traced here: 215 us
  blocking collectives  89.7 us (41%)
  waiting for transfers between devices  78.6 us (36%)
  local copies, waits for them, and re-layouts  26.2 us (12%)
  between operations  13.6 us (6%)
  matrix products  6.39 us (3%)
    all_gather x1, waiting for transfers between devices, body(): lax.all_gather(flat_vectors, 'branch', axis=0, tiled=True)  78.5 us
    psum x1, blocking collectives, body(): top_coeffs = lax.psum(folded, 'leaf').astype(jnp.bfloat16)  47.6 us
    all_gather x1, blocking collectives, body(): lax.all_gather(partial_root, 'branch', axis=0, tiled=True)  42.1 us
    gather x2, local copies, waits for them, and re-layouts, gather_rows(): picked = jnp.take(table, places.reshape(-1), axis=0)  5.81 us
  transfers between devices with their start and end apart: 2, of which 1 were waited for; matrix products, arithmetic and copies ran while one was open for 10% of the time, Pallas kernels for 0%

commit v1 on v0

v1 whole, which is shorter than its diff:
```python
import jax
import jax.numpy as jnp
from jax import lax
from jax.experimental import pallas as pl
from jax.experimental.pallas import tpu as pltpu
from jax.sharding import PartitionSpec as P

LEAF = 64
RANK = 64
RHS = 16
NEAR = 8
COUP = 8
CAP = 4
LEAF_DEV = 16
N_BRANCH = 64
N_LEAF = 16
SLOTS = N_BRANCH * CAP
PAIRS = LEAF // 2
MIB = 1024 * 1024

f32 = jnp.float32
bf16 = jnp.bfloat16
i32 = jnp.int32


def dot(a, b, contract=((1,), (0,))):
    return lax.dot_general(a, b, (contract, ((), ())), preferred_element_type=f32)


def dot_t(a, b):
    return dot(a, b, ((1,), (1,)))


def iota(shape, axis):
    return lax.broadcasted_iota(i32, shape, axis)


def hot(condition):
    return condition.astype(f32).astype(bf16)


def split_rows(source, scratch, count, which):
    return scratch[pl.ds(which, PAIRS, stride=count), :].astype(bf16)


def up_kernel(
    near_ref, coup_ref, vectors_ref, basis_ref, transfer_ref, table_ref, named_ref, out_ref, held_b, held_t
):
    for t in range(PAIRS):
        rows = slice(t * LEAF_DEV, (t + 1) * LEAF_DEV)
        lanes = slice(t * 128, (t + 1) * 128)
        held_b[rows, :] = basis_ref[:, lanes].astype(f32)
        held_t[rows, :] = transfer_ref[:, lanes].astype(f32)
    parity = [hot(iota((LEAF, PAIRS), 0) == 2 * iota((LEAF, PAIRS), 1) + h) for h in range(2)]
    x = jnp.concatenate(
        [vectors_ref[:, l * LEAF : (l + 1) * LEAF] for l in range(LEAF_DEV)], axis=0
    )
    x_parts = [dot(x, m).astype(bf16) for m in parity]
    coeffs = []
    for l in range(LEAF_DEV):
        rows = slice(l * RHS, (l + 1) * RHS)
        both = jnp.concatenate([part[rows] for part in x_parts], axis=0)
        got = dot(both, split_rows(basis_ref, held_b, LEAF_DEV, l))
        c = got[:RHS, :RANK] + got[RHS:, RANK:]
        c = c.astype(bf16)
        coeffs.append(c)
        c = c.astype(f32)
        v = x[rows].astype(f32)
        table_ref[l] = jnp.concatenate([c, c], axis=1)
        table_ref[LEAF_DEV + l] = jnp.concatenate([v, v], axis=1)
    c_all = jnp.concatenate(coeffs, axis=0)
    c_parts = [dot(c_all, m).astype(bf16) for m in parity]
    total = jnp.zeros((2 * RHS, 128), f32)
    for l in range(LEAF_DEV):
        rows = slice(l * RHS, (l + 1) * RHS)
        both = jnp.concatenate([part[rows] for part in c_parts], axis=0)
        total = total + dot(both, split_rows(transfer_ref, held_t, LEAF_DEV, l))
    root = total[:RHS, :RANK] + total[RHS:, RANK:]
    flat = jnp.concatenate([root[: RHS // 2], root[RHS // 2 :]], axis=1)
    high = flat.astype(bf16).astype(f32)
    parts = jnp.concatenate([high, flat - high], axis=0)
    named = jnp.zeros((N_BRANCH, 128), f32)
    for ids_ref in (near_ref, coup_ref):
        for entry in range(NEAR):
            ids = ids_ref[entry : entry + 1, :]
            owner_hot = hot((ids >> 8) == iota((N_BRANCH, LEAF_DEV), 0))
            within_hot = hot((ids & (LEAF_DEV - 1)) == iota((128, LEAF_DEV), 0))
            named = named + dot_t(owner_hot, within_hot)
    named = jnp.minimum(named, 1.0)
    named_ref[...] = named
    for peer in range(N_BRANCH):
        mask = jnp.broadcast_to(named[peer : peer + 1], (8, 128))
        out_ref[peer] = jnp.concatenate([parts, mask], axis=0).astype(bf16)


def prepare_kernel(
    me_ref, near_ref, coup_ref, named_ref, blocks_n, blocks_c, down_ref, basis_ref,
    near_out, coup_out, down_out, basis_out, place_ref, held, held_r,
):
    named = named_ref[...].astype(bf16)
    before = hot(iota((128, 128), 0) < iota((128, 128), 1))
    rank_of = dot(named, before).astype(bf16)
    for which, ids_ref in enumerate((near_ref, coup_ref)):
        for entry in range(NEAR):
            ids = ids_ref[entry : entry + 1, :]
            owner, within = ids >> 8, ids & (LEAF_DEV - 1)
            owner_hot = hot(owner == iota((N_BRANCH, LEAF_DEV), 0))
            rank = dot(rank_of, owner_hot, ((0,), (0,)))
            rank = jnp.where(within == iota((128, LEAF_DEV), 0), rank, 0.0)
            rank = jnp.sum(rank, axis=0, keepdims=True).astype(i32)
            row = which * NEAR + entry
            place_ref[row : row + 1, :] = jnp.where(owner == me_ref[0], SLOTS + within, owner * CAP + rank)
    for source, target in ((down_ref, down_out), (basis_ref, basis_out)):
        for t in range(PAIRS):
            held_r[t * LEAF_DEV : (t + 1) * LEAF_DEV, :] = source[:, t * 128 : (t + 1) * 128].astype(f32)
        for i in range(LEAF_DEV):
            target[i * PAIRS : (i + 1) * PAIRS, :] = split_rows(source, held_r, LEAF_DEV, i)

    def one_leaf(i, carry):
        for side, (source, target) in enumerate(((blocks_n, near_out), (blocks_c, coup_out))):
            for t in range(PAIRS):
                held[side, t * NEAR : (t + 1) * NEAR, :] = source[i, :, t * 128 : (t + 1) * 128].astype(f32)
            for j in range(NEAR):
                target[i, :, j * 128 : (j + 1) * 128] = held[side, pl.ds(j, PAIRS, stride=NEAR), :].astype(bf16)
        return carry

    lax.fori_loop(0, LEAF_DEV, one_leaf, 0)


def pick_kernel(me_ref, incoming_ref, table_ref, prepared_ref, out_ref, shares_ref, index_v, index_s, sem):
    wanted = jnp.max(incoming_ref[...].astype(f32)[:, 16:24, :], axis=1)
    turn = hot(iota((N_BRANCH, 128), 0) == iota((N_BRANCH, 128), 1))
    wanted = dot(wanted.astype(bf16), turn, ((0,), (0,)))
    before = hot(iota((128, 128), 1) < iota((128, 128), 0))
    order = wanted * (dot(before, wanted.astype(bf16)) + 1.0)
    hop = (iota((1, 128), 1) - me_ref[0] + N_BRANCH) % N_BRANCH
    base = jnp.where((hop == 1) | (hop == N_BRANCH - 1), LEAF_DEV, 0)
    leaf = iota((128, 128), 0)
    picks = [
        jnp.sum(jnp.where(order == k + 1.0, leaf, 0), axis=0, keepdims=True) + base for k in range(CAP)
    ]
    index_v[...] = jnp.concatenate(picks + picks, axis=0)
    copy = pltpu.make_async_copy(index_v, index_s, sem)
    copy.start()
    copy.wait()
    left = iota((RHS, 128), 1) < LEAF

    def one_peer(p, carry):
        tiles = [
            jnp.where(left, table_ref[index_s[k, p]], table_ref[index_s[k + 1, p]]) for k in range(0, CAP, 2)
        ]
        out_ref[p] = jnp.concatenate(tiles, axis=0).astype(bf16)
        return carry

    lax.fori_loop(0, N_BRANCH, one_peer, 0, unroll=8)
    for p in range(N_BRANCH):
        parts = incoming_ref[p].astype(f32)
        flat = parts[:8] + parts[8:16]
        shares_ref[p] = jnp.concatenate([flat[:, :RANK], flat[:, RANK:]], axis=0)


def share_kernel(folded_ref, received_ref, out_ref):
    folded = folded_ref[...]
    flat = jnp.concatenate([folded[: RHS // 2], folded[RHS // 2 :]], axis=1)
    out_ref[...] = jnp.broadcast_to(flat[None], out_ref.shape)


def leaves_kernel(place_ref, received_ref, table_ref, near_blocks, coup_blocks, near_out, coup_out, wide):
    lane = iota((RHS, 128), 1)
    half = lane // LEAF
    for i in range(LEAF_DEV):
        for side, (blocks, target) in enumerate(((near_blocks, near_out), (coup_blocks, coup_out))):
            for j in range(NEAR):
                place = place_ref[side * NEAR + j, i]
                tile = received_ref[jnp.minimum(place, SLOTS - 1) // 2].astype(f32)
                tile = jnp.where(half == place % 2, tile, pltpu.roll(tile, LEAF, 1))
                if side == 0:
                    own = table_ref[LEAF_DEV + jnp.maximum(place - SLOTS, 0)]
                    tile = jnp.where(place >= SLOTS, own, tile)
                pair = jnp.concatenate(
                    [jnp.where(half == 0, tile, 0.0), jnp.where(half == 1, tile, 0.0)], axis=0
                )
                wide[i % 2, side, :, j * 128 : (j + 1) * 128] = pair.astype(bf16)
            target[:, i * PAIRS : (i + 1) * PAIRS] = dot_t(wide[i % 2, side], blocks[i])


def down_kernel(shares_ref, near_ref, coup_ref, down_ref, basis_ref, out_ref):
    columns = LEAF_DEV * PAIRS
    top = jnp.sum(shares_ref[...], axis=0)
    top = jnp.concatenate([top[:, :RANK], top[:, RANK:]], axis=0).astype(bf16).astype(f32)
    zero = jnp.zeros((RHS, RANK), f32)
    wide = jnp.concatenate(
        [jnp.concatenate([top, zero], axis=1), jnp.concatenate([zero, top], axis=1)], axis=0
    ).astype(bf16)
    inner = (coup_ref[...] + dot_t(wide, down_ref[...])).astype(bf16)
    block = columns // 2
    order = [
        hot(
            (iota((block, 2 * block), 0) // PAIRS == iota((block, 2 * block), 1) // LEAF)
            & (2 * (iota((block, 2 * block), 0) % PAIRS) + h == iota((block, 2 * block), 1) % LEAF)
        )
        for h in range(2)
    ]

    def in_order(halves):
        return sum(dot(part, m) for part, m in zip(halves, order))

    stacked = [
        jnp.concatenate([inner[h * RHS : (h + 1) * RHS, :block], inner[h * RHS : (h + 1) * RHS, block:]], axis=0)
        for h in range(2)
    ]
    natural = in_order(stacked)
    left = iota((RHS, 128), 1) < LEAF
    pieces = []
    for i in range(LEAF_DEV):
        rows = slice((i // 8) * RHS, (i // 8 + 1) * RHS)
        pair = natural[rows, ((i % 8) // 2) * 128 : ((i % 8) // 2 + 1) * 128]
        other = pltpu.roll(pair, LEAF, 1)
        mine, swapped = (pair, other) if i % 2 == 0 else (other, pair)
        both = jnp.concatenate([jnp.where(left, mine, 0.0), jnp.where(left, 0.0, swapped)], axis=0).astype(bf16)
        pieces.append(dot_t(both, basis_ref[i * PAIRS : (i + 1) * PAIRS, :]))
    result = near_ref[...] + jnp.concatenate(pieces, axis=1)
    high = result.astype(bf16).astype(f32)
    middle = (result - high).astype(bf16).astype(f32)
    parts = [part.astype(bf16) for part in (high, middle, result - high - middle)]
    halves = [
        jnp.concatenate(
            [part[h * RHS : (h + 1) * RHS, b * block : (b + 1) * block] for part in parts for b in range(2)],
            axis=0,
        )
        for h in range(2)
    ]
    ordered = in_order(halves)
    for b in range(2):
        rows = [ordered[(2 * k + b) * RHS : (2 * k + b + 1) * RHS] for k in range(3)]
        out_ref[:, b * 2 * block : (b + 1) * 2 * block] = rows[0] + rows[1] + rows[2]


def body(
    vectors,
    near_ids,
    coup_ids,
    near_blocks,
    coup_blocks,
    col_basis,
    row_basis,
    col_transfer,
    row_transfer,
    top_coupling,
):
    vmem = pl.BlockSpec(memory_space=pltpu.VMEM)
    smem = pl.BlockSpec(memory_space=pltpu.SMEM)
    anywhere = pl.BlockSpec(memory_space=pl.ANY)
    struct = jax.ShapeDtypeStruct

    def params(mib):
        return pltpu.CompilerParams(vmem_limit_bytes=mib * MIB)

    me = lax.axis_index("branch").astype(i32).reshape(1)
    near_t, coup_t = near_ids.T, coup_ids.T

    table, named, outgoing = pl.pallas_call(
        up_kernel,
        out_shape=(
            struct((2 * LEAF_DEV, RHS, 128), f32),
            struct((N_BRANCH, 128), f32),
            struct((N_BRANCH, 24, 128), bf16),
        ),
        in_specs=[vmem] * 5,
        out_specs=(vmem,) * 3,
        scratch_shapes=[pltpu.VMEM((PAIRS * LEAF_DEV, 128), f32)] * 2,
        compiler_params=params(32),
        name="up",
    )(near_t, coup_t, vectors, col_basis, col_transfer)

    incoming = lax.all_to_all(outgoing, "branch", 0, 0, tiled=True)

    wide = NEAR * 128
    near_wide, coup_wide, down_wide, basis_wide, place = pl.pallas_call(
        prepare_kernel,
        out_shape=(
            struct((LEAF_DEV, PAIRS, wide), bf16),
            struct((LEAF_DEV, PAIRS, wide), bf16),
            struct((LEAF_DEV * PAIRS, 128), bf16),
            struct((LEAF_DEV * PAIRS, 128), bf16),
            struct((NEAR + COUP, LEAF_DEV), i32),
        ),
        in_specs=[smem] + [vmem] * 7,
        out_specs=(vmem,) * 5,
        scratch_shapes=[
            pltpu.VMEM((2, PAIRS * NEAR, 128), f32),
            pltpu.VMEM((PAIRS * LEAF_DEV, 128), f32),
        ],
        compiler_params=params(16),
        name="prepare",
    )(me, near_t, coup_t, named, near_blocks, coup_blocks, row_transfer, row_basis)

    sent, shares = pl.pallas_call(
        pick_kernel,
        out_shape=(struct((N_BRANCH, CAP // 2 * RHS, 128), bf16), struct((N_BRANCH, RHS, RANK), f32)),
        in_specs=[smem, vmem, vmem, anywhere],
        out_specs=(vmem, vmem),
        scratch_shapes=[
            pltpu.VMEM((8, 128), i32),
            pltpu.SMEM((8, 128), i32),
            pltpu.SemaphoreType.DMA,
        ],
        compiler_params=params(8),
        name="pick",
    )(me, incoming, table, place)
    received = lax.all_to_all(sent, "branch", 0, 0, tiled=True)

    top_rows = top_coupling.reshape(N_BRANCH, RANK, RANK)
    folded = jnp.einsum("mac,mrc->ra", top_rows, shares, precision=lax.Precision.HIGHEST)
    spread = pl.pallas_call(
        share_kernel,
        out_shape=struct((N_LEAF, 8, 128), f32),
        in_specs=[vmem, anywhere],
        out_specs=vmem,
        compiler_params=params(4),
        name="share",
    )(folded, received)
    gathered = lax.all_to_all(spread, "leaf", 0, 0, tiled=True)

    columns = LEAF_DEV * PAIRS
    near_sum, coup_sum = pl.pallas_call(
        leaves_kernel,
        out_shape=(struct((2 * RHS, columns), f32),) * 2,
        in_specs=[smem] + [vmem] * 4,
        out_specs=(vmem, vmem),
        scratch_shapes=[pltpu.VMEM((2, 2, 2 * RHS, wide), bf16)],
        compiler_params=params(12),
        cost_estimate=pl.CostEstimate(flops=70_000_000, bytes_accessed=4_000_000, transcendentals=0),
        name="leaves",
    )(place, received.reshape(SLOTS // 2, RHS, 128), table, near_wide, coup_wide)

    return pl.pallas_call(
        down_kernel,
        out_shape=struct((RHS, LEAF_DEV * LEAF), f32),
        in_specs=[vmem] * 5,
        out_specs=vmem,
        compiler_params=params(12),
        name="down",
    )(gathered, near_sum, coup_sum, down_wide, basis_wide)


def solution(mesh):
    in_specs = (
        P(None, ("branch", "leaf")),
        P(("branch", "leaf"), None),
        P(("branch", "leaf"), None),
        P(("branch", "leaf"), None, None),
        P(("branch", "leaf"), None, None),
        P(("branch", "leaf"), None),
        P(("branch", "leaf"), None),
        P(("branch", "leaf"), None),
        P(("branch", "leaf"), None),
        P("branch", None, None),
    )
    out_specs = P(None, ("branch", "leaf"))
    return jax.shard_map(body, mesh=mesh, in_specs=in_specs, out_specs=out_specs, check_vma=False)
```

time: 218 us -> 91.3 us (0.42); the launches traced: 215 us -> 90.6 us
  blocking collectives: 89.7 us -> 0 us
  waiting for transfers between devices: 78.6 us -> 17.8 us
  starting transfers between devices: 0.04 us -> 44.2 us
  between operations: 13.6 us -> 0.08 us
  local copies, waits for them, and re-layouts: 26.2 us -> 14.1 us
  Pallas kernels: 0 us -> 11.1 us
  matrix products: 6.39 us -> 3.32 us
    all_gather x2 -> x0, waiting for transfers between devices: 78.5 us -> none  [the longest x1 78.5 us: body(): lax.all_gather(flat_vectors, 'branch', axis=0, tiled=True)]
    psum x1 -> x0, blocking collectives: 47.6 us -> none  [body(): top_coeffs = lax.psum(folded, 'leaf').astype(jnp.bfloat16)]
    all_to_all x0 -> x3, starting transfers between devices: none -> 44.2 us  [the longest x1 23.5 us: body(): gathered = lax.all_to_all(spread, 'leaf', 0, 0, tiled=True)]
    all_gather x1 -> x0, blocking collectives: 42.1 us -> none  [body(): lax.all_gather(partial_root, 'branch', axis=0, tiled=True)]
    all_to_all x0 -> x3, waiting for transfers between devices: none -> 17.8 us  [the longest x1 8.26 us: body(): received = lax.all_to_all(sent, 'branch', 0, 0, tiled=True)]
    reshape x14 -> x1, local copies, waits for them, and re-layouts: 17.8 us -> 3.1 us  [body(): top_rows = top_coupling.reshape(N_BRANCH, RANK, RANK)]
    pallas_call x0 -> x6, Pallas kernels: none -> 11.1 us  [the longest x1 3.76 us: body(): pl.pallas_call(leaves_kernel, out_shape=(struct((2 * RHS, columns), f32),...]
    unnamed x9 -> x28, local copies, waits for them, and re-layouts: 1.01 us -> 11 us
  transfers between devices with their start and end apart: 2 -> 3, of which waited for: 1 -> 3; matrix products, arithmetic and copies ran while one was open for 10% -> 7% of each run, Pallas kernels for 0% -> 6%
where the time goes in v1:
time: 91.3 us; the launch traced here: 90.6 us
  starting transfers between devices  44.2 us (48%)
  waiting for transfers between devices  17.8 us (19%)
  local copies, waits for them, and re-layouts  14.1 us (15%)
  Pallas kernels  11.1 us (12%)
  matrix products  3.32 us (4%)
    all_to_all x1, starting transfers between devices, body(): gathered = lax.all_to_all(spread, 'leaf', 0, 0, tiled=True)  23.5 us
    all_to_all x1, starting transfers between devices, body(): incoming = lax.all_to_all(outgoing, 'branch', 0, 0, tiled=True)  14 us
    unnamed x28, local copies, waits for them, and re-layouts  11 us
    all_to_all x1, waiting for transfers between devices, body(): received = lax.all_to_all(sent, 'branch', 0, 0, tiled=True)  8.26 us
    all_to_all x1, starting transfers between devices, body(): received = lax.all_to_all(sent, 'branch', 0, 0, tiled=True)  6.65 us
    all_to_all x1, waiting for transfers between devices, body(): incoming = lax.all_to_all(outgoing, 'branch', 0, 0, tiled=True)  5.49 us
    all_to_all x1, waiting for transfers between devices, body(): gathered = lax.all_to_all(spread, 'leaf', 0, 0, tiled=True)  4.05 us
    pallas_call x1, Pallas kernels, body(): pl.pallas_call(leaves_kernel, out_shape=(struct((2 * RHS, columns), f32),...  3.76 us
  transfers between devices with their start and end apart: 3, of which 3 were waited for; matrix products, arithmetic and copies ran while one was open for 7% of the time, Pallas kernels for 6%

profile of v1, /device:TPU:1, one launch (start us, length us, event | category | flops | bytes accessed | tf_op | source)
XLA Modules:
  0.0 90.6 jit_solution(6661719284394599157)
XLA Ops:
  0.0 0.0 copy-start.3
  0.0 0.9 copy-done.3
  0.9 0.0 copy-start.4
  0.9 0.9 copy-done.4
  1.8 0.0 copy-start.9
  1.8 0.8 copy-done.9
  2.6 0.0 copy-start.10
  2.6 0.7 copy-done.10
  3.3 0.0 copy-start.12
  3.3 0.7 copy-done.12
  3.9 1.8 %up.1 = (f32[32,16,128]{2,1,0:T(8,128)S(1)}, f32[64,128]{1,0:T(8,128)S(1)}, bf16[64,24,128]{2,1,0:T(8,128)(2,1)}) custom-call(s32[8,16]{1,0:T(8,128)S(1)} %bitcast.9, s32[8,16]{1,0:T(8,128)S(1)} %bitcast.11, bf16[16,1024]{1,0:T(8,128)(2,1)S(1)} %copy-done.9, bf16[16,4096]{1,0:T(8,128)(2,1)S(1)} %copy-done.3, bf16[16,4096]{1,0:T(8,128)(2,1)S(1)} %copy-done.4), custom_call_target="tpu_custom_call" | custom-call | tf_op jit(solution)/shard_map/up/pallas_call | solution.py:262
  5.7 14.0 %all-to-all-start = ((bf16[64,24,128]{2,1,0:T(8,128)(2,1)}), bf16[64,24,128]{2,1,0:T(8,128)(2,1)S(1)}, u32[]{:S(2)}, u32[]{:S(2)}) async-start(bf16[64,24,128]{2,1,0:T(8,128)(2,1)} %get-tuple-element.17), calls=%async_computation | async-start | bytes 786432 | tf_op jit(solution)/shard_map/all_to_all | solution.py:276
  19.7 0.0 copy-start
  19.8 1.2 %copy-done = bf16[16,8,4096]{2,1,0:T(8,128)(2,1)S(1)} copy-done((bf16[16,8,4096]{2,1,0:T(8,128)(2,1)S(1)}, bf16[16,8,4096]{2,1,0:T(8,128)(2,1)}, u32[]{:S(2)}) %copy-start) | copy-done | bytes 1048600
  21.0 0.0 copy-start.1
  21.0 1.2 %copy-done.1 = bf16[16,8,4096]{2,1,0:T(8,128)(2,1)S(1)} copy-done((bf16[16,8,4096]{2,1,0:T(8,128)(2,1)S(1)}, bf16[16,8,4096]{2,1,0:T(8,128)(2,1)}, u32[]{:S(2)}) %copy-start.1) | copy-done | bytes 1048600
  22.2 0.0 copy-start.7
  22.2 0.9 copy-done.7
  23.1 0.0 copy-start.8
  23.1 0.9 copy-done.8
  24.0 0.0 copy-start.11
  24.0 0.7 copy-done.11
  24.7 0.0 copy-start.13
  24.7 0.7 copy-done.13
  25.4 1.8 %prepare.1 = (bf16[16,32,1024]{2,1,0:T(8,128)(2,1)S(1)}, bf16[16,32,1024]{2,1,0:T(8,128)(2,1)S(1)}, bf16[512,128]{1,0:T(8,128)(2,1)S(1)}, bf16[512,128]{1,0:T(8,128)(2,1)S(1)}, s32[16,16]{1,0:T(8,128)S(1)}) custom-call(s32[1]{0:T(128)} %bitcast.me_ref, s32[8,16]{1,0:T(8,128)S(1)} %bitcast.10, s32[8,16]{1,0:T(8,128)S(1)} %bitcast.12, ...), custom_call_target="tpu_custom_call" | custom-call | tf_op jit(solution)/shard_map/prepare/pallas_call | solution.py:279
  27.2 0.0 copy-start.5
  27.2 0.6 copy-done.5
  27.8 5.5 %all-to-all-done.incoming_ref = bf16[64,24,128]{2,1,0:T(8,128)(2,1)S(1)} async-done(((bf16[64,24,128]{2,1,0:T(8,128)(2,1)}), bf16[64,24,128]{2,1,0:T(8,128)(2,1)S(1)}, u32[]{:S(2)}, u32[]{:S(2)}) %all-to-all-start) | async-done | bytes 393248 | tf_op jit(solution)/shard_map/all_to_all | solution.py:276
  33.3 1.6 %pick.1 = (bf16[64,32,128]{2,1,0:T(8,128)(2,1)S(1)}, f32[64,16,64]{2,1,0:T(8,128)S(1)}) custom-call(s32[1]{0:T(128)} %bitcast.me_ref, bf16[64,24,128]{2,1,0:T(8,128)(2,1)S(1)} %all-to-all-done.incoming_ref, f32[32,16,128]{2,1,0:T(8,128)S(1)} %get-tuple-element.18.table_ref, s32[16,16]{1,0:T(8,128)S(1)} %get-tuple-element.20.prepared_ref.place_ref), custom_call_target="tpu_custom_call" | custom-call | tf_op jit(solution)/shard_map/pick/pallas_call | solution.py:298
  34.9 0.0 copy-start.2
  34.9 0.8 copy-done.2
  35.7 6.6 %all-to-all-start.1 = ((bf16[64,32,128]{2,1,0:T(8,128)(2,1)}), bf16[64,32,128]{2,1,0:T(8,128)(2,1)S(1)}, u32[]{:S(2)}, u32[]{:S(2)}) async-start(bf16[64,32,128]{2,1,0:T(8,128)(2,1)} %copy-done.2), calls=%async_computation.1 | async-start | bytes 1048576 | tf_op jit(solution)/shard_map/all_to_all | solution.py:311
  42.3 3.1 %reshape.10 = f32[64,64,64]{2,1,0:T(8,128)} reshape(f32[1,64,4096]{2,1,0:T(8,128)} %param.19) | data formatting | bytes 2097152 | tf_op jit(solution)/shard_map/reshape | solution.py:313
  45.5 3.3 %convolution_bitcast_fusion.folded_ref = f32[16,64]{1,0:T(8,128)S(1)} fusion(f32[64,16,64]{2,1,0:T(8,128)S(1)} %get-tuple-element.21, f32[64,64,64]{2,1,0:T(8,128)} %reshape.10), kind=kOutput, calls=%fused_computation | convolution fusion | flops 50331648 | bytes 1314816 | tf_op jit(solution)/shard_map/mac,mrc->ra/dot_general | solution.py:314
  48.8 0.0 copy-start.6
  48.8 8.3 %all-to-all-done.1.received_ref = bf16[64,32,128]{2,1,0:T(8,128)(2,1)S(1)} async-done(((bf16[64,32,128]{2,1,0:T(8,128)(2,1)}), bf16[64,32,128]{2,1,0:T(8,128)(2,1)S(1)}, u32[]{:S(2)}, u32[]{:S(2)}) %all-to-all-start.1) | async-done | bytes 524320 | tf_op jit(solution)/shard_map/all_to_all | solution.py:311
  57.0 0.7 share.1
  57.7 23.5 %all-to-all-start.2 = ((f32[16,8,128]{2,1,0:T(8,128)}), f32[16,8,128]{2,1,0:T(8,128)S(1)}, u32[]{:S(2)}, u32[]{:S(2)}) async-start(f32[16,8,128]{2,1,0:T(8,128)} %share.1), calls=%async_computation.2 | async-start | bytes 131072 | tf_op jit(solution)/shard_map/all_to_all | solution.py:323
  81.2 3.8 %leaves.1 = (f32[32,512]{1,0:T(8,128)S(1)}, f32[32,512]{1,0:T(8,128)S(1)}) custom-call(s32[16,16]{1,0:T(8,128)S(1)} %get-tuple-element.20.prepared_ref.place_ref, bf16[128,16,128]{2,1,0:T(8,128)(2,1)S(1)} %bitcast.8, f32[32,16,128]{2,1,0:T(8,128)S(1)} %get-tuple-element.18.table_ref, bf16[16,32,1024]{2,1,0:T(8,128)(2,1)S(1)} %get-tuple-element.23.near_blocks, ...), custom_call_target="tpu_custom_call" | custom-call | flops 70000000 | bytes 4000000 | tf_op jit(solution)/shard_map/leaves/pallas_call | solution.py:326
  85.0 4.0 %all-to-all-done.2.shares_ref = f32[16,8,128]{2,1,0:T(8,128)S(1)} async-done(((f32[16,8,128]{2,1,0:T(8,128)}), f32[16,8,128]{2,1,0:T(8,128)S(1)}, u32[]{:S(2)}, u32[]{:S(2)}) %all-to-all-start.2) | async-done | bytes 65568 | tf_op jit(solution)/shard_map/all_to_all | solution.py:323
  89.1 0.0 copy-done.6
  89.1 1.6 %down.1 = f32[16,1024]{1,0:T(8,128)} custom-call(f32[16,8,128]{2,1,0:T(8,128)S(1)} %all-to-all-done.2.shares_ref, f32[32,512]{1,0:T(8,128)S(1)} %get-tuple-element.25.near_ref, f32[32,512]{1,0:T(8,128)S(1)} %get-tuple-element.26.coup_ref, bf16[512,128]{1,0:T(8,128)(2,1)S(1)} %get-tuple-element.27.down_ref, bf16[512,128]{1,0:T(8,128)(2,1)S(1)} %copy-done.6), custom_call_target="tpu_custom_call" | custom-call | tf_op jit(solution)/shard_map/down/pallas_call | solution.py:337
Async XLA Ops:
  0.0 0.9 copy-start.3
  0.9 0.9 copy-start.4
  1.8 0.8 copy-start.9
  2.6 0.7 copy-start.10
  3.3 0.7 copy-start.12
  5.7 27.6 %all-to-all-start = ((bf16[64,24,128]{2,1,0:T(8,128)(2,1)}), bf16[64,24,128]{2,1,0:T(8,128)(2,1)S(1)}, u32[]{:S(2)}, u32[]{:S(2)}) async-start(bf16[64,24,128]{2,1,0:T(8,128)(2,1)} %get-tuple-element.17), calls=%async_computation | async-start | bytes 786432 | tf_op jit(solution)/shard_map/all_to_all | solution.py:276
  19.7 1.2 %copy-start = (bf16[16,8,4096]{2,1,0:T(8,128)(2,1)S(1)}, bf16[16,8,4096]{2,1,0:T(8,128)(2,1)}, u32[]{:S(2)}) copy-start(bf16[16,8,4096]{2,1,0:T(8,128)(2,1)} %blocks_n.1) | copy-start | bytes 3145732
  21.0 1.2 %copy-start.1 = (bf16[16,8,4096]{2,1,0:T(8,128)(2,1)S(1)}, bf16[16,8,4096]{2,1,0:T(8,128)(2,1)}, u32[]{:S(2)}) copy-start(bf16[16,8,4096]{2,1,0:T(8,128)(2,1)} %blocks_c.1) | copy-start | bytes 3145732
  22.2 0.9 copy-start.7
  23.1 0.9 copy-start.8
  24.0 0.7 copy-start.11
  24.7 0.7 copy-start.13
  27.2 0.7 copy-start.5
  34.9 0.8 copy-start.2
  35.7 21.3 %all-to-all-start.1 = ((bf16[64,32,128]{2,1,0:T(8,128)(2,1)}), bf16[64,32,128]{2,1,0:T(8,128)(2,1)S(1)}, u32[]{:S(2)}, u32[]{:S(2)}) async-start(bf16[64,32,128]{2,1,0:T(8,128)(2,1)} %copy-done.2), calls=%async_computation.1 | async-start | bytes 1048576 | tf_op jit(solution)/shard_map/all_to_all | solution.py:311
  48.8 40.3 %copy-start.6 = (bf16[512,128]{1,0:T(8,128)(2,1)S(1)}, bf16[512,128]{1,0:T(8,128)(2,1)}, u32[]{:S(2)}) copy-start(bf16[512,128]{1,0:T(8,128)(2,1)} %copy-done.5) | copy-start | bytes 393220
  57.7 31.3 %all-to-all-start.2 = ((f32[16,8,128]{2,1,0:T(8,128)}), f32[16,8,128]{2,1,0:T(8,128)S(1)}, u32[]{:S(2)}, u32[]{:S(2)}) async-start(f32[16,8,128]{2,1,0:T(8,128)} %share.1), calls=%async_computation.2 | async-start | bytes 131072 | tf_op jit(solution)/shard_map/all_to_all | solution.py:323

commit v2 on v1

--- a/solution.py
+++ b/solution.py
@@ -127,7 +127,9 @@
     lax.fori_loop(0, LEAF_DEV, one_leaf, 0)
 
 
-def pick_kernel(me_ref, incoming_ref, table_ref, prepared_ref, out_ref, shares_ref, index_v, index_s, sem):
+def pick_kernel(
+    me_ref, incoming_ref, table_ref, prepared_ref, top_ref, out_ref, shares_ref, index_v, index_s, sem
+):
     wanted = jnp.max(incoming_ref[...].astype(f32)[:, 16:24, :], axis=1)
     turn = hot(iota((N_BRANCH, 128), 0) == iota((N_BRANCH, 128), 1))
     wanted = dot(wanted.astype(bf16), turn, ((0,), (0,)))
@@ -159,32 +161,37 @@
         shares_ref[p] = jnp.concatenate([flat[:, :RANK], flat[:, RANK:]], axis=0)
 
 
-def share_kernel(folded_ref, received_ref, out_ref):
-    folded = folded_ref[...]
-    flat = jnp.concatenate([folded[: RHS // 2], folded[RHS // 2 :]], axis=1)
-    out_ref[...] = jnp.broadcast_to(flat[None], out_ref.shape)
-
-
-def leaves_kernel(place_ref, received_ref, table_ref, near_blocks, coup_blocks, near_out, coup_out, wide):
-    lane = iota((RHS, 128), 1)
-    half = lane // LEAF
+def finish_kernel(
+    place_ref, shares_ref, received_ref, near_blocks, coup_blocks, table_hbm, down_hbm, basis_hbm, out_ref,
+    own_ref, down_ref, basis_ref, wide, near_ref, coup_ref, sems,
+):
+    def fetch(n, source, target):
+        copy = pltpu.make_async_copy(source, target, sems.at[n])
+        copy.start()
+        return copy
+
+    first = fetch(0, table_hbm.at[pl.ds(LEAF_DEV, LEAF_DEV)], own_ref)
+    last = [fetch(1, down_hbm, down_ref), fetch(2, basis_hbm, basis_ref)]
+    first.wait()
+
+    half = iota((RHS, 128), 1) // LEAF
     for i in range(LEAF_DEV):
-        for side, (blocks, target) in enumerate(((near_blocks, near_out), (coup_blocks, coup_out))):
+        for side, (blocks, target) in enumerate(((near_blocks, near_ref), (coup_blocks, coup_ref))):
             for j in range(NEAR):
                 place = place_ref[side * NEAR + j, i]
                 tile = received_ref[jnp.minimum(place, SLOTS - 1) // 2].astype(f32)
                 tile = jnp.where(half == place % 2, tile, pltpu.roll(tile, LEAF, 1))
                 if side == 0:
-                    own = table_ref[LEAF_DEV + jnp.maximum(place - SLOTS, 0)]
+                    own = own_ref[jnp.maximum(place - SLOTS, 0)]
                     tile = jnp.where(place >= SLOTS, own, tile)
                 pair = jnp.concatenate(
                     [jnp.where(half == 0, tile, 0.0), jnp.where(half == 1, tile, 0.0)], axis=0
                 )
                 wide[i % 2, side, :, j * 128 : (j + 1) * 128] = pair.astype(bf16)
             target[:, i * PAIRS : (i + 1) * PAIRS] = dot_t(wide[i % 2, side], blocks[i])
-
-
-def down_kernel(shares_ref, near_ref, coup_ref, down_ref, basis_ref, out_ref):
+    for copy in last:
+        copy.wait()
+
     columns = LEAF_DEV * PAIRS
     top = jnp.sum(shares_ref[...], axis=0)
     top = jnp.concatenate([top[:, :RANK], top[:, RANK:]], axis=0).astype(bf16).astype(f32)
@@ -254,7 +261,7 @@
     struct = jax.ShapeDtypeStruct
 
     def params(mib):
-        return pltpu.CompilerParams(vmem_limit_bytes=mib * MIB)
+        return pltpu.CompilerParams(vmem_limit_bytes=int(mib * MIB))
 
     me = lax.axis_index("branch").astype(i32).reshape(1)
     near_t, coup_t = near_ids.T, coup_ids.T
@@ -269,7 +276,7 @@
         in_specs=[vmem] * 5,
         out_specs=(vmem,) * 3,
         scratch_shapes=[pltpu.VMEM((PAIRS * LEAF_DEV, 128), f32)] * 2,
-        compiler_params=params(32),
+        compiler_params=params(56),
         name="up",
     )(near_t, coup_t, vectors, col_basis, col_transfer)
 
@@ -291,57 +298,50 @@
             pltpu.VMEM((2, PAIRS * NEAR, 128), f32),
             pltpu.VMEM((PAIRS * LEAF_DEV, 128), f32),
         ],
-        compiler_params=params(16),
+        compiler_params=params(53.5),
         name="prepare",
     )(me, near_t, coup_t, named, near_blocks, coup_blocks, row_transfer, row_basis)
 
+    top_rows = top_coupling.reshape(N_BRANCH, RANK, RANK)
     sent, shares = pl.pallas_call(
         pick_kernel,
         out_shape=(struct((N_BRANCH, CAP // 2 * RHS, 128), bf16), struct((N_BRANCH, RHS, RANK), f32)),
-        in_specs=[smem, vmem, vmem, anywhere],
+        in_specs=[smem, vmem, vmem, anywhere, anywhere],
         out_specs=(vmem, vmem),
         scratch_shapes=[
             pltpu.VMEM((8, 128), i32),
             pltpu.SMEM((8, 128), i32),
             pltpu.SemaphoreType.DMA,
         ],
-        compiler_params=params(8),
+        compiler_params=params(53.3),
         name="pick",
-    )(me, incoming, table, place)
+    )(me, incoming, table, place, top_rows)
     received = lax.all_to_all(sent, "branch", 0, 0, tiled=True)
 
-    top_rows = top_coupling.reshape(N_BRANCH, RANK, RANK)
     folded = jnp.einsum("mac,mrc->ra", top_rows, shares, precision=lax.Precision.HIGHEST)
-    spread = pl.pallas_call(
-        share_kernel,
-        out_shape=struct((N_LEAF, 8, 128), f32),
-        in_specs=[vmem, anywhere],
+    flat = jnp.concatenate([folded[: RHS // 2], folded[RHS // 2 :]], axis=1)
+    gathered = lax.all_gather(flat[None], "leaf", axis=0, tiled=True)
+
+    columns = LEAF_DEV * PAIRS
+    return pl.pallas_call(
+        finish_kernel,
+        out_shape=struct((RHS, LEAF_DEV * LEAF), f32),
+        in_specs=[smem] + [vmem] * 4 + [anywhere] * 3,
         out_specs=vmem,
-        compiler_params=params(4),
-        name="share",
-    )(folded, received)
-    gathered = lax.all_to_all(spread, "leaf", 0, 0, tiled=True)
-
-    columns = LEAF_DEV * PAIRS
-    near_sum, coup_sum = pl.pallas_call(
-        leaves_kernel,
-        out_shape=(struct((2 * RHS, columns), f32),) * 2,
-        in_specs=[smem] + [vmem] * 4,
-        out_specs=(vmem, vmem),
-        scratch_shapes=[pltpu.VMEM((2, 2, 2 * RHS, wide), bf16)],
-        compiler_params=params(12),
-        cost_estimate=pl.CostEstimate(flops=70_000_000, bytes_accessed=4_000_000, transcendentals=0),
-        name="leaves",
-    )(place, received.reshape(SLOTS // 2, RHS, 128), table, near_wide, coup_wide)
-
-    return pl.pallas_call(
-        down_kernel,
-        out_shape=struct((RHS, LEAF_DEV * LEAF), f32),
-        in_specs=[vmem] * 5,
-        out_specs=vmem,
-        compiler_params=params(12),
-        name="down",
-    )(gathered, near_sum, coup_sum, down_wide, basis_wide)
+        scratch_shapes=[
+            pltpu.VMEM((LEAF_DEV, RHS, 128), f32),
+            pltpu.VMEM((columns, 128), bf16),
+            pltpu.VMEM((columns, 128), bf16),
+            pltpu.VMEM((2, 2, 2 * RHS, wide), bf16),
+            pltpu.VMEM((2 * RHS, columns), f32),
+            pltpu.VMEM((2 * RHS, columns), f32),
+            pltpu.SemaphoreType.DMA((3,)),
+        ],
+        compiler_params=params(50),
+        name="finish",
+    )(
+        place, gathered, received.reshape(SLOTS // 2, RHS, 128), near_wide, coup_wide, table, down_wide, basis_wide
+    )
 
 
 def solution(mesh):

time: 91.3 us -> 82 us (0.90)
  blocking collectives: 0 us -> 32.4 us
  starting transfers between devices: 44.2 us -> 20.7 us
  waiting for transfers between devices: 17.8 us -> 5.74 us
  local copies, waits for them, and re-layouts: 14.1 us -> 3.19 us
  Pallas kernels: 11.1 us -> 15.9 us
    all_gather x0 -> x1, blocking collectives: none -> 32.4 us  [body(): gathered = lax.all_gather(flat[None], 'leaf', axis=0, tiled=True)]
    all_to_all x1 -> x0, starting transfers between devices: 23.5 us -> none  [body(): gathered = lax.all_to_all(spread, 'leaf', 0, 0, tiled=True)]
    unnamed x28 -> x14, local copies, waits for them, and re-layouts: 11 us -> 0.03 us
    all_to_all x1, waiting for transfers between devices: 8.26 us -> 0.01 us  [body(): received = lax.all_to_all(sent, 'branch', 0, 0, tiled=True)]
    all_to_all x1 -> x0, waiting for transfers between devices: 4.05 us -> none  [body(): gathered = lax.all_to_all(spread, 'leaf', 0, 0, tiled=True)]
    pallas_call x1, Pallas kernels: 1.78 us -> 4.66 us  [body(): pl.pallas_call(prepare_kernel, out_shape=(struct((LEAF_DEV, PAIRS, wide),...]
    pallas_call x1, Pallas kernels: 1.75 us -> 2.88 us  [body(): pl.pallas_call(up_kernel, out_shape=(struct((2 * LEAF_DEV, RHS, 128), f32...]
    pallas_call x3 -> x1, Pallas kernels: 6.03 us -> 5.88 us  [body(): pl.pallas_call(finish_kernel, out_shape=struct((RHS, LEAF_DEV * LEAF), f3...]
  transfers between devices with their start and end apart: 3 -> 2, of which waited for: 3 -> 1; matrix products, arithmetic and copies ran while one was open for 7% -> 8% of each run, Pallas kernels for 6% -> 6%
where the time goes in v2:
time: 82 us; the launch traced here: 81.6 us
  blocking collectives  32.4 us (40%)
  starting transfers between devices  20.7 us (25%)
  Pallas kernels  15.9 us (19%)
  waiting for transfers between devices  5.74 us (7%)
  matrix products  3.5 us (4%)
  local copies, waits for them, and re-layouts  3.19 us (4%)
    all_gather x1, blocking collectives, body(): gathered = lax.all_gather(flat[None], 'leaf', axis=0, tiled=True)  32.4 us
    all_to_all x1, starting transfers between devices, body(): incoming = lax.all_to_all(outgoing, 'branch', 0, 0, tiled=True)  14.2 us
    all_to_all x1, starting transfers between devices, body(): received = lax.all_to_all(sent, 'branch', 0, 0, tiled=True)  6.55 us
    pallas_call x1, Pallas kernels, body(): pl.pallas_call(finish_kernel, out_shape=struct((RHS, LEAF_DEV * LEAF), f3...  5.88 us
    all_to_all x1, waiting for transfers between devices, body(): incoming = lax.all_to_all(outgoing, 'branch', 0, 0, tiled=True)  5.74 us
    pallas_call x1, Pallas kernels, body(): pl.pallas_call(prepare_kernel, out_shape=(struct((LEAF_DEV, PAIRS, wide),...  4.66 us
    dot_general x1, matrix products, body(): jnp.einsum('mac,mrc->ra', top_rows, shares, precision=lax.Precision.HIGHEST)  3.5 us
    reshape x1, local copies, waits for them, and re-layouts, body(): top_rows = top_coupling.reshape(N_BRANCH, RANK, RANK)  3.16 us
  transfers between devices with their start and end apart: 2, of which 1 were waited for; matrix products, arithmetic and copies ran while one was open for 8% of the time, Pallas kernels for 6%

profile of v2, /device:TPU:1, one launch (start us, length us, event | category | flops | bytes accessed | tf_op | source)
XLA Modules:
  0.0 81.6 jit_solution(8937712750575312427)
XLA Ops:
  0.0 0.0 copy-start.3
  0.0 0.0 copy-start.5
  0.0 0.0 copy-start.6
  0.0 2.9 %up.1 = (f32[32,16,128]{2,1,0:T(8,128)}, f32[64,128]{1,0:T(8,128)}, bf16[64,24,128]{2,1,0:T(8,128)(2,1)}) custom-call(s32[8,16]{1,0:T(8,128)} %bitcast.11, s32[8,16]{1,0:T(8,128)} %bitcast.13, bf16[16,1024]{1,0:T(8,128)(2,1)} %vectors_ref.1, bf16[16,4096]{1,0:T(8,128)(2,1)} %basis_ref.2, bf16[16,4096]{1,0:T(8,128)(2,1)} %transfer_ref.1), custom_call_target="tpu_custom_call" | custom-call | tf_op jit(solution)/shard_map/up/pallas_call | solution.py:269
  2.9 0.0 copy-start.4
  2.9 14.2 %all-to-all-start = ((bf16[64,24,128]{2,1,0:T(8,128)(2,1)}), bf16[64,24,128]{2,1,0:T(8,128)(2,1)S(1)}, u32[]{:S(2)}, u32[]{:S(2)}) async-start(bf16[64,24,128]{2,1,0:T(8,128)(2,1)} %get-tuple-element.17), calls=%async_computation | async-start | bytes 786432 | tf_op jit(solution)/shard_map/all_to_all | solution.py:283
  17.1 0.0 copy-start.2
  17.1 3.2 %reshape.10.top_ref = f32[64,64,64]{2,1,0:T(8,128)} reshape(f32[1,64,4096]{2,1,0:T(8,128)} %param.19) | data formatting | bytes 2097152 | tf_op jit(solution)/shard_map/reshape | solution.py:305
  20.2 0.0 copy-done.3
  20.2 0.0 copy-done.5
  20.2 0.0 copy-done.6
  20.3 0.0 copy-done.4
  20.3 4.7 %prepare.1 = (bf16[16,32,1024]{2,1,0:T(8,128)(2,1)}, bf16[16,32,1024]{2,1,0:T(8,128)(2,1)}, bf16[512,128]{1,0:T(8,128)(2,1)S(1)}, bf16[512,128]{1,0:T(8,128)(2,1)S(1)}, s32[16,16]{1,0:T(8,128)S(1)}) custom-call(s32[1]{0:T(128)} %bitcast.me_ref, s32[8,16]{1,0:T(8,128)S(1)} %bitcast.12, s32[8,16]{1,0:T(8,128)S(1)} %bitcast.14, f32[64,128]{1,0:T(8,128)S(1)} %copy-done.4, ...), custom_call_target="tpu_custom_call" | custom-call | tf_op jit(solution)/shard_map/prepare/pallas_call | solution.py:286
  24.9 5.7 %all-to-all-done.incoming_ref = bf16[64,24,128]{2,1,0:T(8,128)(2,1)S(1)} async-done(((bf16[64,24,128]{2,1,0:T(8,128)(2,1)}), bf16[64,24,128]{2,1,0:T(8,128)(2,1)S(1)}, u32[]{:S(2)}, u32[]{:S(2)}) %all-to-all-start) | async-done | bytes 393248 | tf_op jit(solution)/shard_map/all_to_all | solution.py:283
  30.7 0.0 copy-done.2
  30.7 2.4 %pick.1 = (bf16[64,32,128]{2,1,0:T(8,128)(2,1)}, f32[64,16,64]{2,1,0:T(8,128)}) custom-call(s32[1]{0:T(128)} %bitcast.me_ref, bf16[64,24,128]{2,1,0:T(8,128)(2,1)S(1)} %all-to-all-done.incoming_ref, f32[32,16,128]{2,1,0:T(8,128)S(1)} %copy-done.2, s32[16,16]{1,0:T(8,128)S(1)} %get-tuple-element.16.prepared_ref.place_ref, f32[64,64,64]{2,1,0:T(8,128)} %reshape.10.top_ref), custom_call_target="tpu_custom_call" | custom-call | tf_op jit(solution)/shard_map/pick/pallas_call | solution.py:306
  33.1 0.0 copy-start
  33.1 0.0 copy-start.1
  33.1 6.5 %all-to-all-start.1 = ((bf16[64,32,128]{2,1,0:T(8,128)(2,1)}), bf16[64,32,128]{2,1,0:T(8,128)(2,1)S(1)}, u32[]{:S(2)}, u32[]{:S(2)}) async-start(bf16[64,32,128]{2,1,0:T(8,128)(2,1)} %get-tuple-element.20), calls=%async_computation.1 | async-start | bytes 1048576 | tf_op jit(solution)/shard_map/all_to_all | solution.py:319
  39.7 3.5 %convolution_bitcast_fusion = f32[16,64]{1,0:T(8,128)S(1)} fusion(f32[64,16,64]{2,1,0:T(8,128)} %get-tuple-element.19, f32[64,64,64]{2,1,0:T(8,128)} %reshape.10.top_ref), kind=kOutput, calls=%fused_computation | convolution fusion | flops 50331648 | bytes 1314816 | tf_op jit(solution)/shard_map/mac,mrc->ra/dot_general | solution.py:321
  43.2 0.1 pad_maximum_fusion
  43.3 32.4 %all-gather = f32[128,128]{1,0:T(8,128)S(1)} all-gather(f32[8,128]{1,0:T(8,128)S(1)} %pad_maximum_fusion), channel_id=2, replica_groups=mesh['branch'=64,'leaf'=16] {'leaf'}, dimensions={0}, use_global_device_ids=true | all-gather | bytes 69632 | tf_op jit(solution)/shard_map/all_gather | solution.py:323
  75.7 0.0 all-to-all-done.1
  75.7 0.0 copy-done
  75.7 0.0 copy-done.1
  75.7 5.9 %finish.1 = f32[16,1024]{1,0:T(8,128)} custom-call(s32[16,16]{1,0:T(8,128)S(1)} %get-tuple-element.16.prepared_ref.place_ref, f32[16,8,128]{2,1,0:T(8,128)S(1)} %bitcast.10, bf16[128,16,128]{2,1,0:T(8,128)(2,1)S(1)} %bitcast.9, bf16[16,32,1024]{2,1,0:T(8,128)(2,1)S(1)} %copy-done, bf16[16,32,1024]{2,1,0:T(8,128)(2,1)S(1)} %copy-done.1, ...), custom_call_target="tpu_custom_call" | custom-call | tf_op jit(solution)/shard_map/finish/pallas_call | solution.py:326
  (1 shorter events, 0.0 us)
Async XLA Ops:
  0.0 20.2 %copy-start.3 = (bf16[16,4096]{1,0:T(8,128)(2,1)S(1)}, bf16[16,4096]{1,0:T(8,128)(2,1)}, u32[]{:S(2)}) copy-start(bf16[16,4096]{1,0:T(8,128)(2,1)} %down_ref.1) | copy-start | bytes 393220
  0.0 20.2 %copy-start.5 = (s32[16,8]{0,1:T(8,128)S(1)}, s32[16,8]{0,1:T(8,128)}, u32[]{:S(2)}) copy-start(s32[16,8]{0,1:T(8,128)} %param.11) | copy-start | bytes 1540
  0.0 20.2 %copy-start.6 = (s32[16,8]{0,1:T(8,128)S(1)}, s32[16,8]{0,1:T(8,128)}, u32[]{:S(2)}) copy-start(s32[16,8]{0,1:T(8,128)} %param.12) | copy-start | bytes 1540
  2.9 17.4 %copy-start.4 = (f32[64,128]{1,0:T(8,128)S(1)}, f32[64,128]{1,0:T(8,128)}, u32[]{:S(2)}) copy-start(f32[64,128]{1,0:T(8,128)} %get-tuple-element.15.named_ref) | copy-start | bytes 98308
  2.9 27.8 %all-to-all-start = ((bf16[64,24,128]{2,1,0:T(8,128)(2,1)}), bf16[64,24,128]{2,1,0:T(8,128)(2,1)S(1)}, u32[]{:S(2)}, u32[]{:S(2)}) async-start(bf16[64,24,128]{2,1,0:T(8,128)(2,1)} %get-tuple-element.17), calls=%async_computation | async-start | bytes 786432 | tf_op jit(solution)/shard_map/all_to_all | solution.py:283
  17.1 13.6 %copy-start.2 = (f32[32,16,128]{2,1,0:T(8,128)S(1)}, f32[32,16,128]{2,1,0:T(8,128)}, u32[]{:S(2)}) copy-start(f32[32,16,128]{2,1,0:T(8,128)} %get-tuple-element.18.table_ref.table_hbm) | copy-start | bytes 786436
  33.1 42.6 %copy-start = (bf16[16,32,1024]{2,1,0:T(8,128)(2,1)S(1)}, bf16[16,32,1024]{2,1,0:T(8,128)(2,1)}, u32[]{:S(2)}) copy-start(bf16[16,32,1024]{2,1,0:T(8,128)(2,1)} %get-tuple-element.21.near_blocks) | copy-start | bytes 3145732
  33.1 42.6 %copy-start.1 = (bf16[16,32,1024]{2,1,0:T(8,128)(2,1)S(1)}, bf16[16,32,1024]{2,1,0:T(8,128)(2,1)}, u32[]{:S(2)}) copy-start(bf16[16,32,1024]{2,1,0:T(8,128)(2,1)} %get-tuple-element.22.coup_blocks) | copy-start | bytes 3145732
  33.1 42.6 %all-to-all-start.1 = ((bf16[64,32,128]{2,1,0:T(8,128)(2,1)}), bf16[64,32,128]{2,1,0:T(8,128)(2,1)S(1)}, u32[]{:S(2)}, u32[]{:S(2)}) async-start(bf16[64,32,128]{2,1,0:T(8,128)(2,1)} %get-tuple-element.20), calls=%async_computation.1 | async-start | bytes 1048576 | tf_op jit(solution)/shard_map/all_to_all | solution.py:319

commit v3 on v2

--- a/solution.py
+++ b/solution.py
@@ -16,6 +16,7 @@
 N_LEAF = 16
 SLOTS = N_BRANCH * CAP
 PAIRS = LEAF // 2
+MARK = 128 - LEAF_DEV
 MIB = 1024 * 1024
 
 f32 = jnp.float32
@@ -37,6 +38,10 @@
 
 def hot(condition):
     return condition.astype(f32).astype(bf16)
+
+
+def mask_spot(rows):
+    return (iota((rows, 128), 0) == rows - 1) & (iota((rows, 128), 1) >= MARK)
 
 
 def split_rows(source, scratch, count, which):
@@ -84,13 +89,14 @@
         for entry in range(NEAR):
             ids = ids_ref[entry : entry + 1, :]
             owner_hot = hot((ids >> 8) == iota((N_BRANCH, LEAF_DEV), 0))
-            within_hot = hot((ids & (LEAF_DEV - 1)) == iota((128, LEAF_DEV), 0))
+            within_hot = hot((ids & (LEAF_DEV - 1)) + MARK == iota((128, LEAF_DEV), 0))
             named = named + dot_t(owner_hot, within_hot)
     named = jnp.minimum(named, 1.0)
     named_ref[...] = named
+    spot = mask_spot(RHS)
     for peer in range(N_BRANCH):
-        mask = jnp.broadcast_to(named[peer : peer + 1], (8, 128))
-        out_ref[peer] = jnp.concatenate([parts, mask], axis=0).astype(bf16)
+        mask = jnp.broadcast_to(named[peer : peer + 1], (RHS, 128))
+        out_ref[peer] = jnp.where(spot, mask, parts).astype(bf16)
 
 
 def prepare_kernel(
@@ -106,7 +112,7 @@
             owner, within = ids >> 8, ids & (LEAF_DEV - 1)
             owner_hot = hot(owner == iota((N_BRANCH, LEAF_DEV), 0))
             rank = dot(rank_of, owner_hot, ((0,), (0,)))
-            rank = jnp.where(within == iota((128, LEAF_DEV), 0), rank, 0.0)
+            rank = jnp.where(within + MARK == iota((128, LEAF_DEV), 0), rank, 0.0)
             rank = jnp.sum(rank, axis=0, keepdims=True).astype(i32)
             row = which * NEAR + entry
             place_ref[row : row + 1, :] = jnp.where(owner == me_ref[0], SLOTS + within, owner * CAP + rank)
@@ -130,14 +136,15 @@
 def pick_kernel(
     me_ref, incoming_ref, table_ref, prepared_ref, top_ref, out_ref, shares_ref, index_v, index_s, sem
 ):
-    wanted = jnp.max(incoming_ref[...].astype(f32)[:, 16:24, :], axis=1)
+    spot = mask_spot(8)
+    wanted = jnp.sum(jnp.where(spot[None], incoming_ref[...].astype(f32)[:, 8:16, :], 0.0), axis=1)
     turn = hot(iota((N_BRANCH, 128), 0) == iota((N_BRANCH, 128), 1))
     wanted = dot(wanted.astype(bf16), turn, ((0,), (0,)))
     before = hot(iota((128, 128), 1) < iota((128, 128), 0))
     order = wanted * (dot(before, wanted.astype(bf16)) + 1.0)
     hop = (iota((1, 128), 1) - me_ref[0] + N_BRANCH) % N_BRANCH
     base = jnp.where((hop == 1) | (hop == N_BRANCH - 1), LEAF_DEV, 0)
-    leaf = iota((128, 128), 0)
+    leaf = iota((128, 128), 0) - MARK
     picks = [
         jnp.sum(jnp.where(order == k + 1.0, leaf, 0), axis=0, keepdims=True) + base for k in range(CAP)
     ]
@@ -157,13 +164,13 @@
     lax.fori_loop(0, N_BRANCH, one_peer, 0, unroll=8)
     for p in range(N_BRANCH):
         parts = incoming_ref[p].astype(f32)
-        flat = parts[:8] + parts[8:16]
+        flat = parts[:8] + jnp.where(spot, 0.0, parts[8:])
         shares_ref[p] = jnp.concatenate([flat[:, :RANK], flat[:, RANK:]], axis=0)
 
 
 def finish_kernel(
-    place_ref, shares_ref, received_ref, near_blocks, coup_blocks, table_hbm, down_hbm, basis_hbm, out_ref,
-    own_ref, down_ref, basis_ref, wide, near_ref, coup_ref, sems,
+    place_ref, shares_ref, received_ref, near_blocks, coup_hbm, table_hbm, down_hbm, basis_hbm, out_ref,
+    own_ref, coup_blocks, down_ref, basis_ref, wide, near_ref, coup_ref, sems,
 ):
     def fetch(n, source, target):
         copy = pltpu.make_async_copy(source, target, sems.at[n])
@@ -171,12 +178,15 @@
         return copy
 
     first = fetch(0, table_hbm.at[pl.ds(LEAF_DEV, LEAF_DEV)], own_ref)
+    second = fetch(3, coup_hbm, coup_blocks)
     last = [fetch(1, down_hbm, down_ref), fetch(2, basis_hbm, basis_ref)]
     first.wait()
 
     half = iota((RHS, 128), 1) // LEAF
-    for i in range(LEAF_DEV):
-        for side, (blocks, target) in enumerate(((near_blocks, near_ref), (coup_blocks, coup_ref))):
+    for side, (blocks, target) in enumerate(((near_blocks, near_ref), (coup_blocks, coup_ref))):
+        if side == 1:
+            second.wait()
+        for i in range(LEAF_DEV):
             for j in range(NEAR):
                 place = place_ref[side * NEAR + j, i]
                 tile = received_ref[jnp.minimum(place, SLOTS - 1) // 2].astype(f32)
@@ -271,7 +281,7 @@
         out_shape=(
             struct((2 * LEAF_DEV, RHS, 128), f32),
             struct((N_BRANCH, 128), f32),
-            struct((N_BRANCH, 24, 128), bf16),
+            struct((N_BRANCH, RHS, 128), bf16),
         ),
         in_specs=[vmem] * 5,
         out_specs=(vmem,) * 3,
@@ -326,18 +336,19 @@
     return pl.pallas_call(
         finish_kernel,
         out_shape=struct((RHS, LEAF_DEV * LEAF), f32),
-        in_specs=[smem] + [vmem] * 4 + [anywhere] * 3,
+        in_specs=[smem] + [vmem] * 3 + [anywhere] * 4,
         out_specs=vmem,
         scratch_shapes=[
             pltpu.VMEM((LEAF_DEV, RHS, 128), f32),
+            pltpu.VMEM((LEAF_DEV, PAIRS, wide), bf16),
             pltpu.VMEM((columns, 128), bf16),
             pltpu.VMEM((columns, 128), bf16),
             pltpu.VMEM((2, 2, 2 * RHS, wide), bf16),
             pltpu.VMEM((2 * RHS, columns), f32),
             pltpu.VMEM((2 * RHS, columns), f32),
-            pltpu.SemaphoreType.DMA((3,)),
+            pltpu.SemaphoreType.DMA((4,)),
         ],
-        compiler_params=params(50),
+        compiler_params=params(51),
         name="finish",
     )(
         place, gathered, received.reshape(SLOTS // 2, RHS, 128), near_wide, coup_wide, table, down_wide, basis_wide

time: 82 us -> 80.4 us (0.980)
  blocking collectives: 32.4 us -> 31 us
  starting transfers between devices: 20.7 us -> 21.7 us
  waiting for transfers between devices: 5.74 us -> 4.74 us
    all_gather x1, blocking collectives: 32.4 us -> 31 us  [body(): gathered = lax.all_gather(flat[None], 'leaf', axis=0, tiled=True)]
    all_to_all x1, waiting for transfers between devices: 5.74 us -> 4.74 us  [body(): incoming = lax.all_to_all(outgoing, 'branch', 0, 0, tiled=True)]
    all_to_all x1, starting transfers between devices: 6.55 us -> 7.55 us  [body(): received = lax.all_to_all(sent, 'branch', 0, 0, tiled=True)]
where the time goes in v3:
time: 80.4 us; the launch traced here: 80 us
  blocking collectives  31 us (39%)
  starting transfers between devices  21.7 us (27%)
  Pallas kernels  15.7 us (20%)
  waiting for transfers between devices  4.74 us (6%)
  matrix products  3.5 us (4%)
  local copies, waits for them, and re-layouts  3.17 us (4%)
    all_gather x1, blocking collectives, body(): gathered = lax.all_gather(flat[None], 'leaf', axis=0, tiled=True)  31 us
    all_to_all x1, starting transfers between devices, body(): incoming = lax.all_to_all(outgoing, 'branch', 0, 0, tiled=True)  14.2 us
    all_to_all x1, starting transfers between devices, body(): received = lax.all_to_all(sent, 'branch', 0, 0, tiled=True)  7.55 us
    pallas_call x1, Pallas kernels, body(): pl.pallas_call(finish_kernel, out_shape=struct((RHS, LEAF_DEV * LEAF), f3...  5.79 us
    all_to_all x1, waiting for transfers between devices, body(): incoming = lax.all_to_all(outgoing, 'branch', 0, 0, tiled=True)  4.74 us
    pallas_call x1, Pallas kernels, body(): pl.pallas_call(prepare_kernel, out_shape=(struct((LEAF_DEV, PAIRS, wide),...  4.64 us
    dot_general x1, matrix products, body(): jnp.einsum('mac,mrc->ra', top_rows, shares, precision=lax.Precision.HIGHEST)  3.5 us
    reshape x1, local copies, waits for them, and re-layouts, body(): top_rows = top_coupling.reshape(N_BRANCH, RANK, RANK)  3.14 us
  transfers between devices with their start and end apart: 2, of which 1 were waited for; matrix products, arithmetic and copies ran while one was open for 8% of the time, Pallas kernels for 6%

profile of v3, /device:TPU:1, one launch (start us, length us, event | category | flops | bytes accessed | tf_op | source)
XLA Modules:
  0.0 80.0 jit_solution(14780543204236156571)
XLA Ops:
  0.0 0.0 copy-start.5
  0.0 0.0 copy-start.4
  0.0 0.0 copy-start.2
  0.0 2.8 %up.1 = (f32[32,16,128]{2,1,0:T(8,128)}, f32[64,128]{1,0:T(8,128)}, bf16[64,16,128]{2,1,0:T(8,128)(2,1)}) custom-call(s32[8,16]{1,0:T(8,128)} %bitcast.11, s32[8,16]{1,0:T(8,128)} %bitcast.13, bf16[16,1024]{1,0:T(8,128)(2,1)} %vectors_ref.1, bf16[16,4096]{1,0:T(8,128)(2,1)} %basis_ref.2, bf16[16,4096]{1,0:T(8,128)(2,1)} %transfer_ref.1), custom_call_target="tpu_custom_call" | custom-call | tf_op jit(solution)/shard_map/up/pallas_call | solution.py:279
  2.8 0.0 copy-start.3
  2.8 14.2 %all-to-all-start = ((bf16[64,16,128]{2,1,0:T(8,128)(2,1)}), bf16[64,16,128]{2,1,0:T(8,128)(2,1)S(1)}, u32[]{:S(2)}, u32[]{:S(2)}) async-start(bf16[64,16,128]{2,1,0:T(8,128)(2,1)} %get-tuple-element.17), calls=%async_computation | async-start | bytes 524288 | tf_op jit(solution)/shard_map/all_to_all | solution.py:293
  17.0 0.0 copy-start.1
  17.0 3.1 %reshape.10.top_ref = f32[64,64,64]{2,1,0:T(8,128)} reshape(f32[1,64,4096]{2,1,0:T(8,128)} %param.19) | data formatting | bytes 2097152 | tf_op jit(solution)/shard_map/reshape | solution.py:315
  20.2 0.0 copy-done.5
  20.2 0.0 copy-done.4
  20.2 0.0 copy-done.2
  20.2 0.0 copy-done.3
  20.2 4.6 %prepare.1 = (bf16[16,32,1024]{2,1,0:T(8,128)(2,1)}, bf16[16,32,1024]{2,1,0:T(8,128)(2,1)}, bf16[512,128]{1,0:T(8,128)(2,1)S(1)}, bf16[512,128]{1,0:T(8,128)(2,1)S(1)}, s32[16,16]{1,0:T(8,128)S(1)}) custom-call(s32[1]{0:T(128)} %bitcast.me_ref, s32[8,16]{1,0:T(8,128)S(1)} %bitcast.12, s32[8,16]{1,0:T(8,128)S(1)} %bitcast.14, f32[64,128]{1,0:T(8,128)S(1)} %copy-done.3, ...), custom_call_target="tpu_custom_call" | custom-call | tf_op jit(solution)/shard_map/prepare/pallas_call | solution.py:296
  24.8 4.7 %all-to-all-done.incoming_ref = bf16[64,16,128]{2,1,0:T(8,128)(2,1)S(1)} async-done(((bf16[64,16,128]{2,1,0:T(8,128)(2,1)}), bf16[64,16,128]{2,1,0:T(8,128)(2,1)S(1)}, u32[]{:S(2)}, u32[]{:S(2)}) %all-to-all-start) | async-done | bytes 262176 | tf_op jit(solution)/shard_map/all_to_all | solution.py:293
  29.6 0.0 copy-done.1
  29.6 2.5 %pick.1 = (bf16[64,32,128]{2,1,0:T(8,128)(2,1)}, f32[64,16,64]{2,1,0:T(8,128)}) custom-call(s32[1]{0:T(128)} %bitcast.me_ref, bf16[64,16,128]{2,1,0:T(8,128)(2,1)S(1)} %all-to-all-done.incoming_ref, f32[32,16,128]{2,1,0:T(8,128)S(1)} %copy-done.1, s32[16,16]{1,0:T(8,128)S(1)} %get-tuple-element.16.prepared_ref.place_ref, f32[64,64,64]{2,1,0:T(8,128)} %reshape.10.top_ref), custom_call_target="tpu_custom_call" | custom-call | tf_op jit(solution)/shard_map/pick/pallas_call | solution.py:316
  32.0 0.0 copy-start
  32.0 7.5 %all-to-all-start.1 = ((bf16[64,32,128]{2,1,0:T(8,128)(2,1)}), bf16[64,32,128]{2,1,0:T(8,128)(2,1)S(1)}, u32[]{:S(2)}, u32[]{:S(2)}) async-start(bf16[64,32,128]{2,1,0:T(8,128)(2,1)} %get-tuple-element.20), calls=%async_computation.1 | async-start | bytes 1048576 | tf_op jit(solution)/shard_map/all_to_all | solution.py:329
  39.6 3.5 %convolution_bitcast_fusion = f32[16,64]{1,0:T(8,128)S(1)} fusion(f32[64,16,64]{2,1,0:T(8,128)} %get-tuple-element.19, f32[64,64,64]{2,1,0:T(8,128)} %reshape.10.top_ref), kind=kOutput, calls=%fused_computation | convolution fusion | flops 50331648 | bytes 1314816 | tf_op jit(solution)/shard_map/mac,mrc->ra/dot_general | solution.py:331
  43.1 0.1 pad_maximum_fusion
  43.2 31.0 %all-gather = f32[128,128]{1,0:T(8,128)S(1)} all-gather(f32[8,128]{1,0:T(8,128)S(1)} %pad_maximum_fusion), channel_id=2, replica_groups=mesh['branch'=64,'leaf'=16] {'leaf'}, dimensions={0}, use_global_device_ids=true | all-gather | bytes 69632 | tf_op jit(solution)/shard_map/all_gather | solution.py:333
  74.2 0.0 all-to-all-done.1
  74.2 0.0 copy-done
  74.2 5.8 %finish.1 = f32[16,1024]{1,0:T(8,128)} custom-call(s32[16,16]{1,0:T(8,128)S(1)} %get-tuple-element.16.prepared_ref.place_ref, f32[16,8,128]{2,1,0:T(8,128)S(1)} %bitcast.10, bf16[128,16,128]{2,1,0:T(8,128)(2,1)S(1)} %bitcast.9, bf16[16,32,1024]{2,1,0:T(8,128)(2,1)S(1)} %copy-done, bf16[16,32,1024]{2,1,0:T(8,128)(2,1)} %get-tuple-element.22.coup_hbm, ...), custom_call_target="tpu_custom_call" | custom-call | tf_op jit(solution)/shard_map/finish/pallas_call | solution.py:336
  (1 shorter events, 0.0 us)
Async XLA Ops:
  0.0 20.2 %copy-start.5 = (s32[16,8]{0,1:T(8,128)S(1)}, s32[16,8]{0,1:T(8,128)}, u32[]{:S(2)}) copy-start(s32[16,8]{0,1:T(8,128)} %param.12) | copy-start | bytes 1540
  0.0 20.2 %copy-start.4 = (s32[16,8]{0,1:T(8,128)S(1)}, s32[16,8]{0,1:T(8,128)}, u32[]{:S(2)}) copy-start(s32[16,8]{0,1:T(8,128)} %param.11) | copy-start | bytes 1540
  0.0 20.2 %copy-start.2 = (bf16[16,4096]{1,0:T(8,128)(2,1)S(1)}, bf16[16,4096]{1,0:T(8,128)(2,1)}, u32[]{:S(2)}) copy-start(bf16[16,4096]{1,0:T(8,128)(2,1)} %down_ref.1) | copy-start | bytes 393220
  2.8 17.3 %copy-start.3 = (f32[64,128]{1,0:T(8,128)S(1)}, f32[64,128]{1,0:T(8,128)}, u32[]{:S(2)}) copy-start(f32[64,128]{1,0:T(8,128)} %get-tuple-element.15.named_ref) | copy-start | bytes 98308
  2.8 26.7 %all-to-all-start = ((bf16[64,16,128]{2,1,0:T(8,128)(2,1)}), bf16[64,16,128]{2,1,0:T(8,128)(2,1)S(1)}, u32[]{:S(2)}, u32[]{:S(2)}) async-start(bf16[64,16,128]{2,1,0:T(8,128)(2,1)} %get-tuple-element.17), calls=%async_computation | async-start | bytes 524288 | tf_op jit(solution)/shard_map/all_to_all | solution.py:293
  17.0 12.6 %copy-start.1 = (f32[32,16,128]{2,1,0:T(8,128)S(1)}, f32[32,16,128]{2,1,0:T(8,128)}, u32[]{:S(2)}) copy-start(f32[32,16,128]{2,1,0:T(8,128)} %get-tuple-element.18.table_ref.table_hbm) | copy-start | bytes 786436
  32.0 42.2 %copy-start = (bf16[16,32,1024]{2,1,0:T(8,128)(2,1)S(1)}, bf16[16,32,1024]{2,1,0:T(8,128)(2,1)}, u32[]{:S(2)}) copy-start(bf16[16,32,1024]{2,1,0:T(8,128)(2,1)} %get-tuple-element.21.near_blocks) | copy-start | bytes 3145732
  32.0 42.2 %all-to-all-start.1 = ((bf16[64,32,128]{2,1,0:T(8,128)(2,1)}), bf16[64,32,128]{2,1,0:T(8,128)(2,1)S(1)}, u32[]{:S(2)}, u32[]{:S(2)}) async-start(bf16[64,32,128]{2,1,0:T(8,128)(2,1)} %get-tuple-element.20), calls=%async_computation.1 | async-start | bytes 1048576 | tf_op jit(solution)/shard_map/all_to_all | solution.py:329

commit v4 on v3

--- a/solution.py
+++ b/solution.py
@@ -134,7 +134,7 @@
 
 
 def pick_kernel(
-    me_ref, incoming_ref, table_ref, prepared_ref, top_ref, out_ref, shares_ref, index_v, index_s, sem
+    me_ref, incoming_ref, table_ref, prepared_ref, out_ref, shares_ref, index_v, index_s, sem
 ):
     spot = mask_spot(8)
     wanted = jnp.sum(jnp.where(spot[None], incoming_ref[...].astype(f32)[:, 8:16, :], 0.0), axis=1)
@@ -316,7 +316,7 @@
     sent, shares = pl.pallas_call(
         pick_kernel,
         out_shape=(struct((N_BRANCH, CAP // 2 * RHS, 128), bf16), struct((N_BRANCH, RHS, RANK), f32)),
-        in_specs=[smem, vmem, vmem, anywhere, anywhere],
+        in_specs=[smem, vmem, vmem, anywhere],
         out_specs=(vmem, vmem),
         scratch_shapes=[
             pltpu.VMEM((8, 128), i32),
@@ -325,7 +325,7 @@
         ],
         compiler_params=params(53.3),
         name="pick",
-    )(me, incoming, table, place, top_rows)
+    )(me, incoming, table, place)
     received = lax.all_to_all(sent, "branch", 0, 0, tiled=True)
 
     folded = jnp.einsum("mac,mrc->ra", top_rows, shares, precision=lax.Precision.HIGHEST)

time: 80.4 us -> 82.5 us (1.026)
  local copies, waits for them, and re-layouts: 3.17 us -> 5.22 us
    unnamed x12 -> x16, local copies, waits for them, and re-layouts: 0.02 us -> 3.04 us
    reshape x1, local copies, waits for them, and re-layouts: 3.14 us -> 2.17 us  [body(): top_rows = top_coupling.reshape(N_BRANCH, RANK, RANK)]
  transfers between devices with their start and end apart: 2 -> 2, of which waited for: 1 -> 1; matrix products, arithmetic and copies ran while one was open for 8% -> 7% of each run, Pallas kernels for 6% -> 6%
where the time goes in v4:
time: 82.5 us; the launch traced here: 82 us
  blocking collectives  31 us (38%)
  starting transfers between devices  21.7 us (26%)
  Pallas kernels  15.8 us (19%)
  local copies, waits for them, and re-layouts  5.22 us (6%)
  waiting for transfers between devices  4.78 us (6%)
  matrix products  3.41 us (4%)
    all_gather x1, blocking collectives, body(): gathered = lax.all_gather(flat[None], 'leaf', axis=0, tiled=True)  31 us
    all_to_all x1, starting transfers between devices, body(): incoming = lax.all_to_all(outgoing, 'branch', 0, 0, tiled=True)  14.2 us
    all_to_all x1, starting transfers between devices, body(): received = lax.all_to_all(sent, 'branch', 0, 0, tiled=True)  7.5 us
    pallas_call x1, Pallas kernels, body(): pl.pallas_call(finish_kernel, out_shape=struct((RHS, LEAF_DEV * LEAF), f3...  5.8 us
    all_to_all x1, waiting for transfers between devices, body(): incoming = lax.all_to_all(outgoing, 'branch', 0, 0, tiled=True)  4.78 us
    pallas_call x1, Pallas kernels, body(): pl.pallas_call(prepare_kernel, out_shape=(struct((LEAF_DEV, PAIRS, wide),...  4.73 us
    dot_general x1, matrix products, body(): jnp.einsum('mac,mrc->ra', top_rows, shares, precision=lax.Precision.HIGHEST)  3.41 us
    unnamed x16, local copies, waits for them, and re-layouts  3.04 us
  transfers between devices with their start and end apart: 2, of which 1 were waited for; matrix products, arithmetic and copies ran while one was open for 7% of the time, Pallas kernels for 6%

profile of v4, /device:TPU:1, one launch (start us, length us, event | category | flops | bytes accessed | tf_op | source)
XLA Modules:
  0.0 82.0 jit_solution(1035698965277270057)
XLA Ops:
  0.0 2.8 %up.1 = (f32[32,16,128]{2,1,0:T(8,128)}, f32[64,128]{1,0:T(8,128)}, bf16[64,16,128]{2,1,0:T(8,128)(2,1)}) custom-call(s32[8,16]{1,0:T(8,128)} %bitcast.11, s32[8,16]{1,0:T(8,128)} %bitcast.13, bf16[16,1024]{1,0:T(8,128)(2,1)} %vectors_ref.1, bf16[16,4096]{1,0:T(8,128)(2,1)} %basis_ref.2, bf16[16,4096]{1,0:T(8,128)(2,1)} %transfer_ref.1), custom_call_target="tpu_custom_call" | custom-call | tf_op jit(solution)/shard_map/up/pallas_call | solution.py:279
  2.8 0.0 copy-start.1
  2.8 14.2 %all-to-all-start = ((bf16[64,16,128]{2,1,0:T(8,128)(2,1)}), bf16[64,16,128]{2,1,0:T(8,128)(2,1)S(1)}, u32[]{:S(2)}, u32[]{:S(2)}) async-start(bf16[64,16,128]{2,1,0:T(8,128)(2,1)} %get-tuple-element.17), calls=%async_computation | async-start | bytes 524288 | tf_op jit(solution)/shard_map/all_to_all | solution.py:293
  17.0 0.0 copy-start.2
  17.0 0.9 %copy-done.2 = bf16[16,4096]{1,0:T(8,128)(2,1)S(1)} copy-done((bf16[16,4096]{1,0:T(8,128)(2,1)S(1)}, bf16[16,4096]{1,0:T(8,128)(2,1)}, u32[]{:S(2)}) %copy-start.2) | copy-done | bytes 131096
  17.9 0.0 copy-start.3
  17.9 0.8 copy-done.3
  18.6 0.0 copy-start.4
  18.6 0.7 copy-done.4
  19.3 0.0 copy-start.5
  19.3 0.7 copy-done.5
  20.0 0.0 copy-start.6
  20.0 4.7 %prepare.1 = (bf16[16,32,1024]{2,1,0:T(8,128)(2,1)}, bf16[16,32,1024]{2,1,0:T(8,128)(2,1)}, bf16[512,128]{1,0:T(8,128)(2,1)S(1)}, bf16[512,128]{1,0:T(8,128)(2,1)S(1)}, s32[16,16]{1,0:T(8,128)S(1)}) custom-call(s32[1]{0:T(128)} %bitcast.me_ref, s32[8,16]{1,0:T(8,128)S(1)} %bitcast.12, s32[8,16]{1,0:T(8,128)S(1)} %bitcast.14, f32[64,128]{1,0:T(8,128)S(1)} %copy-done.3, ...), custom_call_target="tpu_custom_call" | custom-call | tf_op jit(solution)/shard_map/prepare/pallas_call | solution.py:296
  24.7 4.8 %all-to-all-done.incoming_ref = bf16[64,16,128]{2,1,0:T(8,128)(2,1)S(1)} async-done(((bf16[64,16,128]{2,1,0:T(8,128)(2,1)}), bf16[64,16,128]{2,1,0:T(8,128)(2,1)S(1)}, u32[]{:S(2)}, u32[]{:S(2)}) %all-to-all-start) | async-done | bytes 262176 | tf_op jit(solution)/shard_map/all_to_all | solution.py:293
  29.5 0.0 copy-done.1
  29.5 2.5 %pick.1 = (bf16[64,32,128]{2,1,0:T(8,128)(2,1)}, f32[64,16,64]{2,1,0:T(8,128)}) custom-call(s32[1]{0:T(128)} %bitcast.me_ref, bf16[64,16,128]{2,1,0:T(8,128)(2,1)S(1)} %all-to-all-done.incoming_ref, f32[32,16,128]{2,1,0:T(8,128)S(1)} %copy-done.1, s32[16,16]{1,0:T(8,128)S(1)} %get-tuple-element.16.prepared_ref.place_ref), custom_call_target="tpu_custom_call" | custom-call | tf_op jit(solution)/shard_map/pick/pallas_call | solution.py:316
  32.0 0.0 copy-start.7
  32.0 7.5 %all-to-all-start.1 = ((bf16[64,32,128]{2,1,0:T(8,128)(2,1)}), bf16[64,32,128]{2,1,0:T(8,128)(2,1)S(1)}, u32[]{:S(2)}, u32[]{:S(2)}) async-start(bf16[64,32,128]{2,1,0:T(8,128)(2,1)} %get-tuple-element.20), calls=%async_computation.1 | async-start | bytes 1048576 | tf_op jit(solution)/shard_map/all_to_all | solution.py:329
  39.5 0.0 copy-done.6
  39.5 2.2 %reshape.10 = f32[64,64,64]{2,1,0:T(8,128)} reshape(f32[1,64,4096]{2,1,0:T(8,128)S(1)} %copy-done.6) | data formatting | bytes 2097152 | tf_op jit(solution)/shard_map/reshape | solution.py:315
  41.7 0.0 copy-start
  41.7 0.0 copy-done.7
  41.7 3.4 %convolution_bitcast_fusion = f32[16,64]{1,0:T(8,128)S(1)} fusion(f32[64,16,64]{2,1,0:T(8,128)S(1)} %copy-done.7, f32[64,64,64]{2,1,0:T(8,128)} %reshape.10), kind=kOutput, calls=%fused_computation | convolution fusion | flops 50331648 | bytes 1314816 | tf_op jit(solution)/shard_map/mac,mrc->ra/dot_general | solution.py:331
  45.1 0.1 pad_maximum_fusion
  45.2 31.0 %all-gather = f32[128,128]{1,0:T(8,128)S(1)} all-gather(f32[8,128]{1,0:T(8,128)S(1)} %pad_maximum_fusion), channel_id=2, replica_groups=mesh['branch'=64,'leaf'=16] {'leaf'}, dimensions={0}, use_global_device_ids=true | all-gather | bytes 69632 | tf_op jit(solution)/shard_map/all_gather | solution.py:333
  76.2 0.0 all-to-all-done.1
  76.2 0.0 copy-done
  76.2 5.8 %finish.1 = f32[16,1024]{1,0:T(8,128)} custom-call(s32[16,16]{1,0:T(8,128)S(1)} %get-tuple-element.16.prepared_ref.place_ref, f32[16,8,128]{2,1,0:T(8,128)S(1)} %bitcast.10, bf16[128,16,128]{2,1,0:T(8,128)(2,1)S(1)} %bitcast.9, bf16[16,32,1024]{2,1,0:T(8,128)(2,1)S(1)} %copy-done, bf16[16,32,1024]{2,1,0:T(8,128)(2,1)} %get-tuple-element.22.coup_hbm, ...), custom_call_target="tpu_custom_call" | custom-call | tf_op jit(solution)/shard_map/finish/pallas_call | solution.py:336
  (1 shorter events, 0.0 us)
Async XLA Ops:
  2.8 26.7 %copy-start.1 = (f32[32,16,128]{2,1,0:T(8,128)S(1)}, f32[32,16,128]{2,1,0:T(8,128)}, u32[]{:S(2)}) copy-start(f32[32,16,128]{2,1,0:T(8,128)} %get-tuple-element.18.table_ref.table_hbm) | copy-start | bytes 786436
  2.8 26.7 %all-to-all-start = ((bf16[64,16,128]{2,1,0:T(8,128)(2,1)}), bf16[64,16,128]{2,1,0:T(8,128)(2,1)S(1)}, u32[]{:S(2)}, u32[]{:S(2)}) async-start(bf16[64,16,128]{2,1,0:T(8,128)(2,1)} %get-tuple-element.17), calls=%async_computation | async-start | bytes 524288 | tf_op jit(solution)/shard_map/all_to_all | solution.py:293
  17.0 0.9 %copy-start.2 = (bf16[16,4096]{1,0:T(8,128)(2,1)S(1)}, bf16[16,4096]{1,0:T(8,128)(2,1)}, u32[]{:S(2)}) copy-start(bf16[16,4096]{1,0:T(8,128)(2,1)} %down_ref.1) | copy-start | bytes 393220
  17.9 0.8 copy-start.3
  18.6 0.7 copy-start.4
  19.3 0.7 copy-start.5
  20.0 19.5 %copy-start.6 = (f32[1,64,4096]{2,1,0:T(8,128)S(1)}, f32[1,64,4096]{2,1,0:T(8,128)}, u32[]{:S(2)}) copy-start(f32[1,64,4096]{2,1,0:T(8,128)} %param.19) | copy-start | bytes 3145732
  32.0 9.7 %copy-start.7 = (f32[64,16,64]{2,1,0:T(8,128)S(1)}, f32[64,16,64]{2,1,0:T(8,128)}, u32[]{:S(2)}) copy-start(f32[64,16,64]{2,1,0:T(8,128)} %get-tuple-element.19) | copy-start | bytes 786436
  32.0 44.2 %all-to-all-start.1 = ((bf16[64,32,128]{2,1,0:T(8,128)(2,1)}), bf16[64,32,128]{2,1,0:T(8,128)(2,1)S(1)}, u32[]{:S(2)}, u32[]{:S(2)}) async-start(bf16[64,32,128]{2,1,0:T(8,128)(2,1)} %get-tuple-element.20), calls=%async_computation.1 | async-start | bytes 1048576 | tf_op jit(solution)/shard_map/all_to_all | solution.py:329
  41.7 34.5 %copy-start = (bf16[16,32,1024]{2,1,0:T(8,128)(2,1)S(1)}, bf16[16,32,1024]{2,1,0:T(8,128)(2,1)}, u32[]{:S(2)}) copy-start(bf16[16,32,1024]{2,1,0:T(8,128)(2,1)} %get-tuple-element.21.near_blocks) | copy-start | bytes 3145732
